TPU v7x, 768 devices: a whole 4x8x12 slice. The times are simulated.
768 devices in a mesh: dp: 96 (over z, y_lo, x), mp: 8 (over y_hi, core).
Axes of the slice: x: 4, y: 8 (y_hi: 4, y_lo: 2; y = y_hi * 2 + y_lo), z: 12, core: 2. Of those that a mesh axis runs over, the one named last changes fastest.
Arguments:
- tokens: bfloat16 [49152, 3072], P(('dp', 'mp')), parts along dimension 0, may hold values from -6 to 6
- ln_gain: float32 [3072], replicated, may hold values from 0.5 to 1.5
- w_in: bfloat16 [3072, 9216], P(None, 'mp'), may hold values from -0.108253175 to 0.108253175
- qk_gain: float32 [2, 24, 128], P(None, 'mp'), may hold values from 0.45 to 6
- w_out: bfloat16 [3072, 3072], P('mp'), may hold values from -0.109375 to 0.109375
Outputs:
- block_out: bfloat16 [49152, 3072], P(('dp', 'mp')), parts along dimension 0
There are 96 independent parts, one for each index of `dp`. A program takes and returns all parts, laid end to end along the dimension named above; an argument that names none is the same for every part. Nothing has to cross between parts.
All inputs are finite; a program needn't handle non-finite values.
Results may differ from a plain program's by a relative error of at most 0.015.
Values may be sent and summed in bfloat16 or wider, within the bound.
No kernel may reach another device: no remote copies, remote signals or barrier semaphores. Data moves between devices by JAX's collectives and lax.ppermute only.
A program may use at most 32 MiB of HBM per device.

v0:
```python
import math

import jax
import jax.numpy as jnp
from jax import lax
from jax.sharding import PartitionSpec as P

PATCHES = 256


EPSILON = 1e-06


def layer_norm(entries, gain_row):
    average = jnp.mean(entries, axis=-1, keepdims=True)
    centred = entries - average
    spread = jnp.mean(centred * centred, axis=-1, keepdims=True)
    return centred * lax.rsqrt(spread + EPSILON) * gain_row


def attend(queries, key_rows, value_rows, head_size):
    images = queries.shape[0] // PATCHES
    left = queries.reshape(images, PATCHES, -1, head_size)
    right = key_rows.reshape(images, PATCHES, -1, head_size)
    carried = value_rows.reshape(images, PATCHES, -1, head_size)
    scores = jnp.einsum(
        "iphd,iqhd->ihpq", left, right, preferred_element_type=jnp.float32
    ) / math.sqrt(head_size)
    largest = jnp.max(scores, axis=-1, keepdims=True)
    raised = jnp.exp(scores - largest)
    denominator = jnp.sum(raised, axis=-1, keepdims=True)
    weights = (raised / denominator).astype(jnp.bfloat16)
    mixed = jnp.einsum("ihpq,iqhd->iphd", weights, carried, preferred_element_type=jnp.float32)
    return mixed.reshape(queries.shape[0], -1).astype(jnp.bfloat16)


def body(tokens, ln_gain, w_in, qk_gain, w_out):
    heads_here = qk_gain.shape[1]
    head_size = qk_gain.shape[2]
    head_cols = heads_here * head_size
    own_rows = tokens.shape[0]
    total_rows = own_rows * lax.axis_size("mp")
    source = layer_norm(tokens.astype(jnp.float32), ln_gain).astype(jnp.bfloat16)
    projected = jnp.dot(
        lax.all_gather(source, "mp", axis=0, tiled=True), w_in, preferred_element_type=jnp.float32
    )
    queries = layer_norm(
        projected[:, :head_cols].reshape(total_rows, heads_here, head_size), qk_gain[0]
    ).astype(jnp.bfloat16)
    key_rows = layer_norm(
        projected[:, head_cols : 2 * head_cols].reshape(total_rows, heads_here, head_size),
        qk_gain[1],
    ).astype(jnp.bfloat16)
    value_rows = (
        projected[:, 2 * head_cols : 3 * head_cols]
        .reshape(total_rows, heads_here, head_size)
        .astype(jnp.bfloat16)
    )
    joined = attend(queries, key_rows, value_rows, head_size)
    branch = lax.psum_scatter(
        jnp.dot(joined, w_out, preferred_element_type=jnp.float32).astype(jnp.bfloat16),
        "mp",
        scatter_dimension=0,
        tiled=True,
    ).astype(jnp.float32)
    return (tokens.astype(jnp.float32) + branch).astype(jnp.bfloat16)


def solution(mesh):
    return jax.shard_map(
        body,
        mesh=mesh,
        in_specs=(P(("dp", "mp"), None), P(), P(None, "mp"), P(None, "mp", None), P("mp", None)),
        out_specs=P(("dp", "mp"), None),
        check_vma=False,
    )
```

profile of v0, /device:TPU:2, one launch (start us, length us, event | category | flops | bytes accessed | tf_op | source)
XLA Modules:
  0.0 165.5 jit_solution(8826953693668098210)
XLA Ops:
  6.5 0.0 copy-start
  6.5 0.0 all-gather.2.cloned.1.call-start
  6.5 1.3 convert_reduce_fusion
  7.9 1.3 fusion.6
  9.1 1.9 %fusion.8 = bf16[64,3072]{1,0:T(8,128)(2,1)} fusion(bf16[64,3072]{1,0:T(8,128)(2,1)} %param.5, f32[3072]{0:T(1024)} %param.6, f32[64]{0:T(128)S(1)} %add_rsqrt_fusion.2, f32[64]{0:T(128)S(1)} %broadcast_multiply_fusion.2), kind=kLoop, calls=%fused_computation.15 | loop fusion | flops 983040 | bytes 799232 | tf_op jit(solution)/shard_map/convert_element_type | solution.py:43
  11.1 0.0 all-gather.2.cloned.1.call-update
  11.1 0.0 reduce-scatter.2.cloned.1.call-start
  11.1 0.8 fusion.24
  11.9 0.6 copy_bitcast_fusion
  12.5 55.0 %all-gather.2.cloned.1.call-done = bf16[512,3072]{1,0:T(8,128)(2,1)} async-done(((bf16[64,3072]{1,0:T(8,128)(2,1)}), bf16[512,3072]{1,0:T(8,128)(2,1)}) %all-gather.2.cloned.1.call-update) | async-done | bytes 3145744 | tf_op jit(solution)/shard_map/all_gather | solution.py:45
  67.6 8.2 %fusion.30 = f32[512,1152]{1,0:T(8,128)S(1)} fusion(bf16[512,3072]{1,0:T(8,128)(2,1)} %all-gather.2.cloned.1.call-done, bf16[3072,1152]{1,0:T(8,128)(2,1)} %param.7), kind=kOutput, calls=%fused_computation.38 | convolution fusion | flops 3623878656 | bytes 12582912 | tf_op jit(solution)/shard_map/dot_general | solution.py:44
  75.7 0.0 copy-start.3
  75.7 1.3 fusion.23
  77.1 0.5 copy-done.3
  77.6 1.4 copy.11
  79.0 0.1 reduce_sum.65
  79.1 0.1 multiply_reduce_fusion.1
  79.2 0.6 div.39
  79.8 1.4 reshape.85
  81.2 1.4 copy.13
  82.6 0.1 reduce_sum.67
  82.7 0.1 multiply_reduce_fusion
  82.8 0.6 div.42
  83.4 1.4 reshape.87
  84.8 0.0 copy-start.2
  84.8 1.3 slice.25
  86.0 0.6 add_rsqrt_fusion.1
  86.6 1.3 rsqrt.32
  88.0 0.9 reshape.89
  88.9 1.7 %multiply_convert_fusion.1 = bf16[2,256,3,128]{1,0,3,2:T(2,128)(2,1)S(1)} fusion(f32[2,256,3,128]{1,0,3,2:T(2,128)} %reshape.85, f32[3,128]{1,0:T(4,128)} %get-tuple-element.12, f32[2,256,3]{1,0,2:T(2,128)} %rsqrt.32, f32[2,256,3]{1,0,2:T(2,128)} %div.39), kind=kLoop, calls=%fused_computation.20 | loop fusion | flops 786432 | bytes 1193472 | tf_op jit(solution)/shard_map/convert_element_type | solution.py:49
  90.6 0.0 copy-done.2
  90.6 2.0 %multiply_convert_fusion = bf16[2,256,3,128]{1,0,3,2:T(2,128)(2,1)} fusion(f32[2,256,3,128]{1,0,3,2:T(2,128)S(1)} %copy-done.2, f32[3,128]{1,0:T(4,128)} %get-tuple-element.11, f32[2,256,3]{1,0,2:T(2,128)S(1)} %rsqrt.34, f32[2,256,3]{1,0,2:T(2,128)} %div.42), kind=kLoop, calls=%fused_computation.18 | loop fusion | flops 786432 | bytes 1193472 | tf_op jit(solution)/shard_map/convert_element_type | solution.py:53
  92.5 2.8 %fusion.25 = (f32[2,3,256]{2,1,0:T(4,128)S(1)}, f32[2,3,256,256]{2,3,1,0:T(8,128)}) fusion(bf16[2,256,3,128]{1,0,3,2:T(2,128)(2,1)} %multiply_convert_fusion, bf16[2,256,3,128]{1,0,3,2:T(2,128)(2,1)S(1)} %multiply_convert_fusion.1), kind=kOutput, calls=%fused_computation.37 | convolution fusion | flops 101843200 | bytes 2365440 | tf_op jit(solution)/shard_map/sub | solution.py:30
  95.4 1.9 %fusion.3 = bf16[2,256,3,128]{1,3,2,0:T(8,128)(2,1)S(1)} fusion(f32[2,3,256,256]{2,3,1,0:T(8,128)} %get-tuple-element.10, f32[2,3,256]{2,1,0:T(4,128)S(1)} %get-tuple-element.9, bf16[2,256,3,128]{3,2,1,0:T(4,128)(2,1)} %reshape.89), kind=kOutput, calls=%fused_computation.7 | convolution fusion | flops 101646336 | bytes 2365440 | tf_op jit(solution)/shard_map/ihpq,iqhd->iphd/dot_general | solution.py:33
  97.3 0.4 copy.19
  97.7 0.1 copy.25
  97.7 0.0 copy-done
  97.7 3.5 %convolution_convert_fusion = bf16[512,3072]{1,0:T(8,128)(2,1)} fusion(bf16[512,384]{0,1:T(8,128)(2,1)S(1)} %bitcast.34, bf16[384,3072]{1,0:T(8,128)(2,1)S(1)} %copy-done), kind=kOutput, calls=%fused_computation.1 | convolution fusion | flops 1209532416 | bytes 5898240 | tf_op jit(solution)/shard_map/dot_general | solution.py:61
  101.3 0.0 copy-start.1
  101.3 0.0 reduce-scatter.2.cloned.1.call-update
  101.3 55.6 %reduce-scatter.2.cloned.1.call-done = bf16[64,3072]{1,0:T(8,128)(2,1)} async-done(((bf16[512,3072]{1,0:T(8,128)(2,1)}), bf16[64,3072]{1,0:T(8,128)(2,1)}) %reduce-scatter.2.cloned.1.call-update) | async-done | bytes 393232 | tf_op jit(solution)/shard_map/reduce_scatter | solution.py:60
  156.8 0.0 copy-done.1
  156.8 1.8 %fusion.9 = bf16[64,3072]{1,0:T(8,128)(2,1)} fusion(bf16[64,3072]{1,0:T(8,128)(2,1)S(1)} %copy-done.1, bf16[64,3072]{1,0:T(8,128)(2,1)} %reduce-scatter.2.cloned.1.call-done), kind=kLoop, calls=%fused_computation.16 | loop fusion | flops 786432 | bytes 1179648 | tf_op jit(solution)/shard_map/convert_element_type | solution.py:66
  (6 shorter events, 0.0 us)
Async XLA Ops:
  6.5 91.2 %copy-start = (bf16[384,3072]{1,0:T(8,128)(2,1)S(1)}, bf16[384,3072]{1,0:T(8,128)(2,1)}, u32[]{:S(2)}) copy-start(bf16[384,3072]{1,0:T(8,128)(2,1)} %param.9) | copy-start | bytes 7077892
  6.5 61.0 %all-gather.2.cloned.1.call-start = ((), (), s32[]{:S(2)}) async-start(), calls=%async_computation.1 | async-start | bytes 3538944 | tf_op jit(solution)/shard_map/all_gather | solution.py:45
  11.1 145.7 %reduce-scatter.2.cloned.1.call-start = ((), (), s32[]{:S(2)}) async-start(), calls=%async_computation.2 | async-start | bytes 3538944 | tf_op jit(solution)/shard_map/reduce_scatter | solution.py:60
  75.7 1.9 %copy-start.3 = (f32[512,1152]{1,0:T(8,128)}, f32[512,1152]{1,0:T(8,128)S(1)}, u32[]{:S(2)}) copy-start(f32[512,1152]{1,0:T(8,128)S(1)} %fusion.30) | copy-start | bytes 7077892
  84.8 5.8 %copy-start.2 = (f32[2,256,3,128]{1,0,3,2:T(2,128)S(1)}, f32[2,256,3,128]{1,0,3,2:T(2,128)}, u32[]{:S(2)}) copy-start(f32[2,256,3,128]{1,0,3,2:T(2,128)} %reshape.87) | copy-start | bytes 2359300
  101.3 55.6 %copy-start.1 = (bf16[64,3072]{1,0:T(8,128)(2,1)S(1)}, bf16[64,3072]{1,0:T(8,128)(2,1)}, u32[]{:S(2)}) copy-start(bf16[64,3072]{1,0:T(8,128)(2,1)} %param.5) | copy-start | bytes 1179652
Sparse Core Ops, SparseCore 0:
  11.2 56.2 all-gather.1
  101.4 55.3 reduce-scatter.1
where the time goes:
time: 166 us
  waiting for transfers between devices  111 us (67%)
  matrix products  16.4 us (10%)
  local copies, waits for them, and re-layouts  14 us (8%)
  between operations  13.5 us (8%)
  other arithmetic  10.9 us (7%)
    reduce_scatter x1, waiting for transfers between devices, body(): lax.psum_scatter(jnp.dot(joined, w_out, preferred_element_type=jnp.float3...  55.6 us
    all_gather x1, waiting for transfers between devices, body(): lax.all_gather(source, 'mp', axis=0, tiled=True)  55 us
    dot_general x1, matrix products, body(): jnp.dot(lax.all_gather(source, 'mp', axis=0, tiled=True), w_in, preferred...  8.18 us
    dot_general x1, matrix products, body(): jnp.dot(joined, w_out, preferred_element_type=jnp.float32)  3.52 us
  transfers between devices with their start and end apart: 2, of which 2 were waited for; matrix products, arithmetic and copies ran while one was open for 1% of the time, Pallas kernels for 0%

commit v1 on v0

v1 whole, which is shorter than its diff:
```python
import math

import jax
import jax.numpy as jnp
from jax import lax
from jax.experimental import pallas as pl
from jax.experimental.pallas import tpu as pltpu
from jax.sharding import PartitionSpec as P

EPSILON = 1e-06
CHIPS = 4
CORES = 2


def place(chip, core):
    return (chip % CHIPS) * CORES + core


NEAR_A = [
    (place(0, 0), place(1, 0)), (place(0, 1), place(3, 0)), (place(1, 0), place(0, 0)), (place(1, 1), place(2, 0)),
    (place(2, 0), place(3, 1)), (place(2, 1), place(1, 1)), (place(3, 0), place(2, 1)), (place(3, 1), place(0, 1)),
]
NEAR_B = [
    (place(0, 0), place(3, 0)), (place(0, 1), place(1, 0)), (place(1, 0), place(2, 0)), (place(1, 1), place(0, 0)),
    (place(2, 0), place(1, 1)), (place(2, 1), place(3, 1)), (place(3, 0), place(0, 1)), (place(3, 1), place(2, 1)),
]
SAME = [(place(0, 1), place(0, 0)), (place(1, 1), place(1, 0)), (place(2, 0), place(2, 1)), (place(3, 0), place(3, 1))]
FAR_A = [(place(1, 0), place(2, 0)), (place(0, 0), place(3, 0)), (place(3, 1), place(0, 1)), (place(2, 1), place(1, 1))]
FAR_B = [(place(3, 0), place(2, 0)), (place(2, 0), place(3, 0)), (place(1, 1), place(0, 1)), (place(0, 1), place(1, 1))]
SWAP = [(i, i ^ 1) for i in range(CHIPS * CORES)]


def back(pairs):
    return [(target, source) for source, target in pairs]


def send(value, pairs):
    return lax.ppermute(value, "mp", pairs)


def normalize(entries, gain):
    average = jnp.mean(entries, axis=-1, keepdims=True)
    centred = entries - average
    spread = jnp.mean(centred * centred, axis=-1, keepdims=True)
    return centred * lax.rsqrt(spread + EPSILON) * gain


def norm_rows(ref, gain_ref, normed, at):
    step = 16

    @pl.loop(0, ref.shape[0] // step)
    def _(i):
        entries = ref[pl.ds(pl.multiple_of(i * step, step), step), :].astype(jnp.float32)
        normed[pl.ds(pl.multiple_of(at + i * step, step), step), :] = normalize(entries, gain_ref[...]).astype(
            jnp.bfloat16
        )


def project(normed, w_ref, projected, top, left):
    rows, width = normed.shape[0], w_ref.shape[1]
    for start in range(0, width, 256):
        size = min(256, width - start)
        projected[top : top + rows, left + start : left + start + size] = jnp.dot(
            normed[...], w_ref[:, start : start + size], preferred_element_type=jnp.float32
        )


def out_terms(joined, w_ref, w2_ref, upper_ref, lower_ref):
    half, block = w_ref.shape[0], upper_ref.shape[0]
    for start in range(0, upper_ref.shape[1], 512):
        columns = slice(start, start + 512)
        term = jnp.dot(joined[:, :half], w_ref[:, columns], preferred_element_type=jnp.float32) + jnp.dot(
            joined[:, half:], w2_ref[:, columns], preferred_element_type=jnp.float32
        )
        upper_ref[:, columns] = term[:block].astype(jnp.bfloat16)
        lower_ref[:, columns] = term[block:].astype(jnp.bfloat16)


def near_kernel(a_ref, b_ref, gain_ref, w_hbm, w2_hbm, wo_hbm, wo2_hbm, w_ref, w2_ref, wo_ref, wo2_ref, projected, normed, sems):
    loads = [
        pltpu.make_async_copy(source, target, sems.at[i])
        for i, (source, target) in enumerate(((w_hbm, w_ref), (w2_hbm, w2_ref), (wo_hbm, wo_ref), (wo2_hbm, wo2_ref)))
    ]
    for load in loads:
        load.start()
    norm_rows(a_ref, gain_ref, normed, 0)
    norm_rows(b_ref, gain_ref, normed, a_ref.shape[0])
    loads[0].wait()
    project(normed, w_ref, projected, 0, 0)
    loads[1].wait()
    project(normed, w2_ref, projected, 0, w_ref.shape[1])
    loads[2].wait()
    loads[3].wait()


def attention_kernel(
    local_ref, own_ref, same_ref, far_a_ref, far_b_ref, gain_ref, qk_ref, qk2_ref, w_ref, w2_ref, wo_ref, wo2_ref,
    near_ref, joined_ref, third_ref, fourth_ref, normed, projected, joined,
):
    block = own_ref.shape[0]
    heads, head_size = qk_ref.shape[1:]

    @pl.when(local_ref[0] == 1)
    def _():
        norm_rows(same_ref, gain_ref, normed, 0)
        norm_rows(own_ref, gain_ref, normed, block)

    @pl.when(local_ref[0] == 0)
    def _():
        norm_rows(far_a_ref, gain_ref, normed, 0)
        norm_rows(far_b_ref, gain_ref, normed, block)

    width = w_ref.shape[1]
    project(normed, w_ref, projected, 0, 0)
    project(normed, w2_ref, projected, 0, width)

    for index, ref in ((0, qk_ref), (1, qk2_ref)):
        for head in range(heads):
            def part(kind):
                at = index * width + (kind * heads + head) * head_size
                return jnp.concatenate([near_ref[:, at : at + head_size], projected[:, at : at + head_size]], axis=0)

            queries = normalize(part(0), ref[0, head : head + 1, :]).astype(jnp.bfloat16)
            keys = normalize(part(1), ref[1, head : head + 1, :]).astype(jnp.bfloat16)
            values = part(2).astype(jnp.bfloat16)
            scores = lax.dot_general(
                queries, keys, (((1,), (1,)), ((), ())), preferred_element_type=jnp.float32
            ) * (1.0 / math.sqrt(head_size))
            raised = jnp.exp(scores - jnp.max(scores, axis=-1, keepdims=True))
            weights = (raised * (1.0 / jnp.sum(raised, axis=-1, keepdims=True))).astype(jnp.bfloat16)
            mixed = jnp.dot(weights, values, preferred_element_type=jnp.float32).astype(jnp.bfloat16)
            at = (index * heads + head) * head_size
            joined_ref[:, at : at + head_size] = mixed[: 2 * block]
            joined[:, at : at + head_size] = mixed[2 * block :]

    out_terms(joined, wo_ref, wo2_ref, third_ref, fourth_ref)


def output_kernel(joined_ref, wo_ref, wo2_ref, first_ref, second_ref):
    out_terms(joined_ref, wo_ref, wo2_ref, first_ref, second_ref)


def whole(count, space=pltpu.VMEM):
    return [pl.BlockSpec(memory_space=space)] * count


def held(value):
    return pltpu.with_memory_space_constraint(value, pltpu.VMEM)


def stored(value):
    return pltpu.with_memory_space_constraint(value, pltpu.HBM)


def body(tokens, ln_gain, w_in, qk_gain, w_out):
    block, width = tokens.shape
    heads, head_size = qk_gain.shape[1:]
    me = lax.axis_index("mp")
    local = (me // (CHIPS // 2 * CORES)) == (me % CORES)
    gain = ln_gain.reshape(1, width)

    near_a = send(tokens, NEAR_A)
    near_b = send(tokens, NEAR_B)
    w_in2 = send(w_in, SWAP)
    w_out2 = send(w_out, SWAP)
    qk_gain2 = send(qk_gain, SWAP)
    same = send(tokens, SAME)
    far_a = send(near_a, FAR_A)
    far_b = send(near_a, FAR_B)

    row_block = jax.ShapeDtypeStruct((block, width), jnp.bfloat16)
    w_vmem, w2_vmem, wo_vmem, wo2_vmem, projected = pl.pallas_call(
        near_kernel,
        out_shape=(
            pltpu.VMEM(w_in.shape, jnp.bfloat16),
            pltpu.VMEM(w_in.shape, jnp.bfloat16),
            pltpu.VMEM(w_out.shape, jnp.bfloat16),
            pltpu.VMEM(w_out.shape, jnp.bfloat16),
            pltpu.VMEM((2 * block, 2 * w_in.shape[1]), jnp.float32),
        ),
        in_specs=whole(3) + whole(4, pl.ANY),
        out_specs=tuple(whole(5)),
        scratch_shapes=[pltpu.VMEM((2 * block, width), jnp.bfloat16), pltpu.SemaphoreType.DMA((4,))],
        compiler_params=pltpu.CompilerParams(vmem_limit_bytes=12 * 1024 * 1024),
        cost_estimate=pl.CostEstimate(flops=2_000_000_000, bytes_accessed=19_000_000, transcendentals=0),
    )(stored(near_a), stored(near_b), gain, stored(w_in), stored(w_in2), stored(w_out), stored(w_out2))
    w_vmem, w2_vmem, wo_vmem, wo2_vmem, projected = (
        held(value) for value in (w_vmem, w2_vmem, wo_vmem, wo2_vmem, projected)
    )
    joined, third, fourth = pl.pallas_call(
        attention_kernel,
        out_shape=(jax.ShapeDtypeStruct((2 * block, 2 * heads * head_size), jnp.bfloat16), row_block, row_block),
        in_specs=whole(1, pltpu.SMEM) + whole(12),
        out_specs=tuple(whole(3)),
        scratch_shapes=[
            pltpu.VMEM((2 * block, width), jnp.bfloat16),
            pltpu.VMEM((2 * block, 2 * w_in.shape[1]), jnp.float32),
            pltpu.VMEM((2 * block, 2 * heads * head_size), jnp.bfloat16),
        ],
        compiler_params=pltpu.CompilerParams(vmem_limit_bytes=16 * 1024 * 1024),
        cost_estimate=pl.CostEstimate(flops=4_000_000_000, bytes_accessed=3_000_000, transcendentals=400_000),
    )(
        local.astype(jnp.int32).reshape(1), stored(tokens), stored(same), stored(far_a), stored(far_b), gain, qk_gain,
        qk_gain2, w_vmem, w2_vmem, wo_vmem, wo2_vmem, projected,
    )
    to_far_a = send(third, back(FAR_A) + back(SAME))
    to_far_b = send(fourth, back(FAR_B))
    first, second = pl.pallas_call(
        output_kernel,
        out_shape=(row_block, row_block),
        in_specs=whole(3),
        out_specs=tuple(whole(2)),
        compiler_params=pltpu.CompilerParams(vmem_limit_bytes=8 * 1024 * 1024),
        cost_estimate=pl.CostEstimate(flops=600_000_000, bytes_accessed=1_000_000, transcendentals=0),
    )(joined, wo_vmem, wo2_vmem)
    to_near_b = send(second, back(NEAR_B))
    wide = lambda value: value.astype(jnp.float32)
    passed = (wide(first) + wide(jnp.where(local, to_far_a, to_far_b))).astype(jnp.bfloat16)
    to_near_a = send(passed, back(NEAR_A))
    kept = wide(tokens) + wide(jnp.where(local, fourth, to_far_a)) + wide(to_near_b)
    return (kept + wide(to_near_a)).astype(jnp.bfloat16)


def solution(mesh):
    return jax.shard_map(
        body,
        mesh=mesh,
        in_specs=(P(("dp", "mp"), None), P(), P(None, "mp"), P(None, "mp", None), P("mp", None)),
        out_specs=P(("dp", "mp"), None),
        check_vma=False,
    )
```

time: 166 us -> 88.7 us (0.53)
  the two profiles are of different devices: /device:TPU:2 before, /device:TPU:699 now
where the time goes in v1:
time: 88.7 us; the launch traced here: 88.2 us
  waiting for transfers between devices  37.9 us (43%)
  starting transfers between devices  30.6 us (34%)
  Pallas kernels  16 us (18%)
  local copies, waits for them, and re-layouts  2.25 us (3%)
  other arithmetic  1.15 us (1%)
    ppermute x12, waiting for transfers between devices, send(): return lax.ppermute(value, 'mp', pairs)  37.9 us
    ppermute x12, starting transfers between devices, send(): return lax.ppermute(value, 'mp', pairs)  30.6 us
    pallas_call x1, Pallas kernels, body(): pl.pallas_call(near_kernel, out_shape=(pltpu.VMEM(w_in.shape, jnp.bfloat1...  7.51 us
    pallas_call x1, Pallas kernels, body(): pl.pallas_call(attention_kernel, out_shape=(jax.ShapeDtypeStruct((2 * blo...  7.51 us
    unnamed x13, local copies, waits for them, and re-layouts  2.25 us
  transfers between devices with their start and end apart: 12, of which 3 were waited for; matrix products, arithmetic and copies ran while one was open for 1% of the time, Pallas kernels for 10%

profile of v1, /device:TPU:699, one launch (start us, length us, event | category | flops | bytes accessed | tf_op | source)
XLA Modules:
  0.0 88.2 jit_solution(14989650727962561804)
XLA Ops:
  0.0 2.6 %collective-permute-start.6 = (bf16[3072,1152]{1,0:T(8,128)(2,1)}, bf16[3072,1152]{1,0:T(8,128)(2,1)}, u32[]{:S(2)}, u32[]{:S(2)}) collective-permute-start(bf16[3072,1152]{1,0:T(8,128)(2,1)} %w_hbm.1), channel_id=1, source_target_pairs={{0,1},{1,0},{2,3},{3,2},{4,5},{5,4},{6,7},{7,6},{8,9},{9,8},{10,11... | collective-permute-start | bytes 21233672 | tf_op jit(solution)/shard_map/ppermute | solution.py:38
  2.6 1.9 %collective-permute-start.7 = (bf16[384,3072]{1,0:T(8,128)(2,1)}, bf16[384,3072]{1,0:T(8,128)(2,1)S(1)}, u32[]{:S(2)}, u32[]{:S(2)}) collective-permute-start(bf16[384,3072]{1,0:T(8,128)(2,1)} %wo_hbm.1), channel_id=1, source_target_pairs={{0,1},{1,0},{2,3},{3,2},{4,5},{5,4},{6,7},{7,6},{8,9},{9,8},{10,11... | collective-permute-start | bytes 7077896 | tf_op jit(solution)/shard_map/ppermute | solution.py:38
  4.5 2.4 %collective-permute-start.1 = (bf16[64,3072]{1,0:T(8,128)(2,1)}, bf16[64,3072]{1,0:T(8,128)(2,1)S(1)}, u32[]{:S(2)}, u32[]{:S(2)}) collective-permute-start(bf16[64,3072]{1,0:T(8,128)(2,1)} %own_ref.1), channel_id=1, source_target_pairs={{0,2},{1,6},{2,0},{3,4},{4,7},{5,3},{6,5},{7,1},{8,10},{9,14},{10,... | collective-permute-start | bytes 1179656 | tf_op jit(solution)/shard_map/ppermute | solution.py:38
  6.9 4.2 %collective-permute-start.5 = (bf16[64,3072]{1,0:T(8,128)(2,1)}, bf16[64,3072]{1,0:T(8,128)(2,1)}, u32[]{:S(2)}, u32[]{:S(2)}) collective-permute-start(bf16[64,3072]{1,0:T(8,128)(2,1)} %own_ref.1), channel_id=1, source_target_pairs={{0,6},{1,2},{2,4},{3,0},{4,3},{5,7},{6,1},{7,5},{8,14},{9,10},{10,... | collective-permute-start | bytes 1179656 | tf_op jit(solution)/shard_map/ppermute | solution.py:38
  11.2 1.3 %collective-permute-start = (bf16[64,3072]{1,0:T(8,128)(2,1)}, bf16[64,3072]{1,0:T(8,128)(2,1)S(1)}, u32[]{:S(2)}, u32[]{:S(2)}) collective-permute-start(bf16[64,3072]{1,0:T(8,128)(2,1)} %own_ref.1), channel_id=1, source_target_pairs={{1,0},{3,2},{4,5},{6,7},{9,8},{11,10},{12,13},{14,15},{17,16},{19,... | collective-permute-start | bytes 1179656 | tf_op jit(solution)/shard_map/ppermute | solution.py:38
  12.5 14.3 %collective-permute-done.1.a_ref = bf16[64,3072]{1,0:T(8,128)(2,1)S(1)} collective-permute-done((bf16[64,3072]{1,0:T(8,128)(2,1)}, bf16[64,3072]{1,0:T(8,128)(2,1)S(1)}, u32[]{:S(2)}, u32[]{:S(2)}) %collective-permute-start.1) | collective-permute-done | bytes 393248 | tf_op jit(solution)/shard_map/ppermute | solution.py:38
  26.8 0.0 copy-start.4
  26.8 1.4 %collective-permute-start.2 = (bf16[64,3072]{1,0:T(8,128)(2,1)S(1)}, bf16[64,3072]{1,0:T(8,128)(2,1)S(1)}, u32[]{:S(2)}, u32[]{:S(2)}) collective-permute-start(bf16[64,3072]{1,0:T(8,128)(2,1)S(1)} %collective-permute-done.1.a_ref), channel_id=1, source_target_pairs={{2,4},{0,6},{7,1},{5,3},{10,12},{8,14},{15,9},{13,11},{18,20},{16,... | collective-permute-start | bytes 1179656 | tf_op jit(solution)/shard_map/ppermute | solution.py:38
  28.2 0.0 collective-permute-done.5.b_ref
  28.2 1.4 %collective-permute-start.3 = (bf16[64,3072]{1,0:T(8,128)(2,1)S(1)}, bf16[64,3072]{1,0:T(8,128)(2,1)}, u32[]{:S(2)}, u32[]{:S(2)}) collective-permute-start(bf16[64,3072]{1,0:T(8,128)(2,1)S(1)} %collective-permute-done.1.a_ref), channel_id=1, source_target_pairs={{6,4},{4,6},{3,1},{1,3},{14,12},{12,14},{11,9},{9,11},{22,20},{20,... | collective-permute-start | bytes 1179656 | tf_op jit(solution)/shard_map/ppermute | solution.py:38
  29.6 0.7 copy.7.qk_ref
  30.3 0.0 collective-permute-done.7.wo2_hbm
  30.3 0.0 copy-start.1
  30.3 5.1 %collective-permute-start.4 = (f32[2,3,128]{2,1,0:T(4,128)S(1)}, f32[2,3,128]{2,1,0:T(4,128)S(1)}, u32[]{:S(2)}, u32[]{:S(2)}) collective-permute-start(f32[2,3,128]{2,1,0:T(4,128)S(1)} %copy.7.qk_ref), channel_id=1, source_target_pairs={{0,1},{1,0},{2,3},{3,2},{4,5},{5,4},{6,7},{7,6},{8,9},{9,8},{10,11... | collective-permute-start | bytes 9224 | tf_op jit(solution)/shard_map/ppermute | solution.py:38
  35.4 0.0 collective-permute-done.6.w2_hbm
  35.4 0.0 copy-done.4
  35.4 0.0 copy-done.1
  35.5 0.0 copy-start
  35.5 0.7 copy-done
  36.2 7.5 %shard_map.55 = (bf16[3072,1152]{1,0:T(8,128)(2,1)S(1)}, bf16[3072,1152]{1,0:T(8,128)(2,1)S(1)}, bf16[384,3072]{1,0:T(8,128)(2,1)S(1)}, bf16[384,3072]{1,0:T(8,128)(2,1)S(1)}, f32[128,2304]{1,0:T(8,128)S(1)}) custom-call(bf16[64,3072]{1,0:T(8,128)(2,1)} %copy-done.4, bf16[64,3072]{1,0:T(8,128)(2,1)} %collective-permute-done.5.b_ref, f32[1,3072]{1,0:T(1,128)S(1)} %bitcast.2, ...), custom_call_target="tpu_custom_call" | custom-call | flops 2000000000 | bytes 19000000 | tf_op jit(solution)/shard_map/pallas_call | solution.py:172
  43.7 0.0 collective-permute-done.4.qk2_ref
  43.7 0.0 collective-permute-done.same_ref
  43.7 0.0 copy-start.3
  43.7 0.0 collective-permute-done.2.far_a_ref
  43.7 0.0 copy-start.5
  43.7 0.0 collective-permute-done.3.far_b_ref
  43.7 0.7 copy-done.3
  44.5 0.1 copy-done.5
  44.6 7.5 %shard_map.56 = (bf16[128,768]{1,0:T(8,128)(2,1)S(1)}, bf16[64,3072]{1,0:T(8,128)(2,1)S(1)}, bf16[64,3072]{1,0:T(8,128)(2,1)S(1)}) custom-call(s32[1]{0:T(128)} %bitcast.local_ref, bf16[64,3072]{1,0:T(8,128)(2,1)} %own_ref.1, bf16[64,3072]{1,0:T(8,128)(2,1)} %copy-done.3, bf16[64,3072]{1,0:T(8,128)(2,1)} %copy-done.5, ...), custom_call_target="tpu_custom_call" | custom-call | flops 4000000000 | bytes 3000000 | tf_op jit(solution)/shard_map/pallas_call | solution.py:190
  52.1 0.7 collective-permute-start.10
  52.8 4.3 %collective-permute-start.8 = (bf16[64,3072]{1,0:T(8,128)(2,1)S(1)}, bf16[64,3072]{1,0:T(8,128)(2,1)S(1)}, u32[]{:S(2)}, u32[]{:S(2)}) collective-permute-start(bf16[64,3072]{1,0:T(8,128)(2,1)S(1)} %get-tuple-element.21), channel_id=1, source_target_pairs={{4,2},{6,0},{1,7},{3,5},{0,1},{2,3},{5,4},{7,6},{12,10},{14,8},{9,... | collective-permute-start | bytes 1179656 | tf_op jit(solution)/shard_map/ppermute | solution.py:38
  57.1 0.0 copy-start.2
  57.1 1.0 %shard_map.57 = (bf16[64,3072]{1,0:T(8,128)(2,1)S(1)}, bf16[64,3072]{1,0:T(8,128)(2,1)S(1)}) custom-call(bf16[128,768]{1,0:T(8,128)(2,1)S(1)} %get-tuple-element.22.joined_ref, bf16[384,3072]{1,0:T(8,128)(2,1)S(1)} %get-tuple-element.17.wo_ref, bf16[384,3072]{1,0:T(8,128)(2,1)S(1)} %get-tuple-element.18.wo2_ref), custom_call_target="tpu_custom_call" | custom-call | flops 600000000 | bytes 1000000 | tf_op jit(solution)/shard_map/pallas_call | solution.py:208
  58.1 3.4 %collective-permute-start.9 = (bf16[64,3072]{1,0:T(8,128)(2,1)S(1)}, bf16[64,3072]{1,0:T(8,128)(2,1)S(1)}, u32[]{:S(2)}, u32[]{:S(2)}) collective-permute-start(bf16[64,3072]{1,0:T(8,128)(2,1)S(1)} %get-tuple-element.23), channel_id=1, source_target_pairs={{6,0},{2,1},{4,2},{0,3},{3,4},{7,5},{1,6},{5,7},{14,8},{10,9},{12,... | collective-permute-start | bytes 1179656 | tf_op jit(solution)/shard_map/ppermute | solution.py:38
  61.5 0.0 collective-permute-done.10
  61.5 10.7 %collective-permute-done.8 = bf16[64,3072]{1,0:T(8,128)(2,1)S(1)} collective-permute-done((bf16[64,3072]{1,0:T(8,128)(2,1)S(1)}, bf16[64,3072]{1,0:T(8,128)(2,1)S(1)}, u32[]{:S(2)}, u32[]{:S(2)}) %collective-permute-start.8) | collective-permute-done | bytes 393248 | tf_op jit(solution)/shard_map/ppermute | solution.py:38
  72.2 0.2 add_convert_fusion.1
  72.4 1.9 %collective-permute-start.11 = (bf16[64,3072]{1,0:T(8,128)(2,1)S(1)}, bf16[64,3072]{1,0:T(8,128)(2,1)S(1)}, u32[]{:S(2)}, u32[]{:S(2)}) collective-permute-start(bf16[64,3072]{1,0:T(8,128)(2,1)S(1)} %add_convert_fusion.1), channel_id=1, source_target_pairs={{2,0},{6,1},{0,2},{4,3},{7,4},{3,5},{5,6},{1,7},{10,8},{14,9},{8,1... | collective-permute-start | bytes 1179656 | tf_op jit(solution)/shard_map/ppermute | solution.py:38
  74.3 0.0 collective-permute-done.9
  74.3 12.8 %collective-permute-done.11 = bf16[64,3072]{1,0:T(8,128)(2,1)S(1)} collective-permute-done((bf16[64,3072]{1,0:T(8,128)(2,1)S(1)}, bf16[64,3072]{1,0:T(8,128)(2,1)S(1)}, u32[]{:S(2)}, u32[]{:S(2)}) %collective-permute-start.11) | collective-permute-done | bytes 393248 | tf_op jit(solution)/shard_map/ppermute | solution.py:38
  87.2 0.0 copy-done.2
  87.2 1.0 %add_convert_fusion = bf16[64,3072]{1,0:T(8,128)(2,1)} fusion(bf16[64,3072]{1,0:T(8,128)(2,1)S(1)} %collective-permute-done.11, bf16[64,3072]{1,0:T(8,128)(2,1)S(1)} %collective-permute-done.9, bf16[64,3072]{1,0:T(8,128)(2,1)S(1)} %copy-done.2, bf16[64,3072]{1,0:T(8,128)(2,1)S(1)} %get-tuple-element.20, bf16[64,3072]{1,0:T(8,128)(2,1)S(1)} %collective-permute-done.8, ...), kind=kLoop, calls=%fused_computation | loop fusion | flops 1769472 | bytes 2359297 | tf_op jit(solution)/shard_map/convert_element_type | solution.py:221
Async XLA Ops:
  0.0 35.4 %collective-permute-start.6 = (bf16[3072,1152]{1,0:T(8,128)(2,1)}, bf16[3072,1152]{1,0:T(8,128)(2,1)}, u32[]{:S(2)}, u32[]{:S(2)}) collective-permute-start(bf16[3072,1152]{1,0:T(8,128)(2,1)} %w_hbm.1), channel_id=1, source_target_pairs={{0,1},{1,0},{2,3},{3,2},{4,5},{5,4},{6,7},{7,6},{8,9},{9,8},{10,11... | collective-permute-start | bytes 21233672 | tf_op jit(solution)/shard_map/ppermute | solution.py:38
  2.6 27.7 %collective-permute-start.7 = (bf16[384,3072]{1,0:T(8,128)(2,1)}, bf16[384,3072]{1,0:T(8,128)(2,1)S(1)}, u32[]{:S(2)}, u32[]{:S(2)}) collective-permute-start(bf16[384,3072]{1,0:T(8,128)(2,1)} %wo_hbm.1), channel_id=1, source_target_pairs={{0,1},{1,0},{2,3},{3,2},{4,5},{5,4},{6,7},{7,6},{8,9},{9,8},{10,11... | collective-permute-start | bytes 7077896 | tf_op jit(solution)/shard_map/ppermute | solution.py:38
  4.5 22.3 %collective-permute-start.1 = (bf16[64,3072]{1,0:T(8,128)(2,1)}, bf16[64,3072]{1,0:T(8,128)(2,1)S(1)}, u32[]{:S(2)}, u32[]{:S(2)}) collective-permute-start(bf16[64,3072]{1,0:T(8,128)(2,1)} %own_ref.1), channel_id=1, source_target_pairs={{0,2},{1,6},{2,0},{3,4},{4,7},{5,3},{6,5},{7,1},{8,10},{9,14},{10,... | collective-permute-start | bytes 1179656 | tf_op jit(solution)/shard_map/ppermute | solution.py:38
  6.9 21.3 %collective-permute-start.5 = (bf16[64,3072]{1,0:T(8,128)(2,1)}, bf16[64,3072]{1,0:T(8,128)(2,1)}, u32[]{:S(2)}, u32[]{:S(2)}) collective-permute-start(bf16[64,3072]{1,0:T(8,128)(2,1)} %own_ref.1), channel_id=1, source_target_pairs={{0,6},{1,2},{2,4},{3,0},{4,3},{5,7},{6,1},{7,5},{8,14},{9,10},{10,... | collective-permute-start | bytes 1179656 | tf_op jit(solution)/shard_map/ppermute | solution.py:38
  11.2 32.5 %collective-permute-start = (bf16[64,3072]{1,0:T(8,128)(2,1)}, bf16[64,3072]{1,0:T(8,128)(2,1)S(1)}, u32[]{:S(2)}, u32[]{:S(2)}) collective-permute-start(bf16[64,3072]{1,0:T(8,128)(2,1)} %own_ref.1), channel_id=1, source_target_pairs={{1,0},{3,2},{4,5},{6,7},{9,8},{11,10},{12,13},{14,15},{17,16},{19,... | collective-permute-start | bytes 1179656 | tf_op jit(solution)/shard_map/ppermute | solution.py:38
  26.8 8.6 %copy-start.4 = (bf16[64,3072]{1,0:T(8,128)(2,1)}, bf16[64,3072]{1,0:T(8,128)(2,1)S(1)}, u32[]{:S(2)}) copy-start(bf16[64,3072]{1,0:T(8,128)(2,1)S(1)} %collective-permute-done.1.a_ref) | copy-start | bytes 1179652
  26.8 16.9 %collective-permute-start.2 = (bf16[64,3072]{1,0:T(8,128)(2,1)S(1)}, bf16[64,3072]{1,0:T(8,128)(2,1)S(1)}, u32[]{:S(2)}, u32[]{:S(2)}) collective-permute-start(bf16[64,3072]{1,0:T(8,128)(2,1)S(1)} %collective-permute-done.1.a_ref), channel_id=1, source_target_pairs={{2,4},{0,6},{7,1},{5,3},{10,12},{8,14},{15,9},{13,11},{18,20},{16,... | collective-permute-start | bytes 1179656 | tf_op jit(solution)/shard_map/ppermute | solution.py:38
  28.2 15.5 %collective-permute-start.3 = (bf16[64,3072]{1,0:T(8,128)(2,1)S(1)}, bf16[64,3072]{1,0:T(8,128)(2,1)}, u32[]{:S(2)}, u32[]{:S(2)}) collective-permute-start(bf16[64,3072]{1,0:T(8,128)(2,1)S(1)} %collective-permute-done.1.a_ref), channel_id=1, source_target_pairs={{6,4},{4,6},{3,1},{1,3},{14,12},{12,14},{11,9},{9,11},{22,20},{20,... | collective-permute-start | bytes 1179656 | tf_op jit(solution)/shard_map/ppermute | solution.py:38
  30.3 5.1 %copy-start.1 = (bf16[384,3072]{1,0:T(8,128)(2,1)}, bf16[384,3072]{1,0:T(8,128)(2,1)S(1)}, u32[]{:S(2)}) copy-start(bf16[384,3072]{1,0:T(8,128)(2,1)S(1)} %collective-permute-done.7.wo2_hbm) | copy-start | bytes 7077892
  30.3 13.4 %collective-permute-start.4 = (f32[2,3,128]{2,1,0:T(4,128)S(1)}, f32[2,3,128]{2,1,0:T(4,128)S(1)}, u32[]{:S(2)}, u32[]{:S(2)}) collective-permute-start(f32[2,3,128]{2,1,0:T(4,128)S(1)} %copy.7.qk_ref), channel_id=1, source_target_pairs={{0,1},{1,0},{2,3},{3,2},{4,5},{5,4},{6,7},{7,6},{8,9},{9,8},{10,11... | collective-permute-start | bytes 9224 | tf_op jit(solution)/shard_map/ppermute | solution.py:38
  35.5 0.7 copy-start
  43.7 0.7 copy-start.3
  43.7 0.9 copy-start.5
  52.1 9.4 %collective-permute-start.10 = (bf16[64,3072]{1,0:T(8,128)(2,1)S(1)}, bf16[64,3072]{1,0:T(8,128)(2,1)S(1)}, u32[]{:S(2)}, u32[]{:S(2)}) collective-permute-start(bf16[64,3072]{1,0:T(8,128)(2,1)S(1)} %get-tuple-element.20), channel_id=1, source_target_pairs={{4,6},{6,4},{1,3},{3,1},{12,14},{14,12},{9,11},{11,9},{20,22},{22,... | collective-permute-start | bytes 1179656 | tf_op jit(solution)/shard_map/ppermute | solution.py:38
  52.8 19.4 %collective-permute-start.8 = (bf16[64,3072]{1,0:T(8,128)(2,1)S(1)}, bf16[64,3072]{1,0:T(8,128)(2,1)S(1)}, u32[]{:S(2)}, u32[]{:S(2)}) collective-permute-start(bf16[64,3072]{1,0:T(8,128)(2,1)S(1)} %get-tuple-element.21), channel_id=1, source_target_pairs={{4,2},{6,0},{1,7},{3,5},{0,1},{2,3},{5,4},{7,6},{12,10},{14,8},{9,... | collective-permute-start | bytes 1179656 | tf_op jit(solution)/shard_map/ppermute | solution.py:38
  57.1 30.1 %copy-start.2 = (bf16[64,3072]{1,0:T(8,128)(2,1)S(1)}, bf16[64,3072]{1,0:T(8,128)(2,1)}, u32[]{:S(2)}) copy-start(bf16[64,3072]{1,0:T(8,128)(2,1)} %own_ref.1) | copy-start | bytes 1179652
  58.1 16.2 %collective-permute-start.9 = (bf16[64,3072]{1,0:T(8,128)(2,1)S(1)}, bf16[64,3072]{1,0:T(8,128)(2,1)S(1)}, u32[]{:S(2)}, u32[]{:S(2)}) collective-permute-start(bf16[64,3072]{1,0:T(8,128)(2,1)S(1)} %get-tuple-element.23), channel_id=1, source_target_pairs={{6,0},{2,1},{4,2},{0,3},{3,4},{7,5},{1,6},{5,7},{14,8},{10,9},{12,... | collective-permute-start | bytes 1179656 | tf_op jit(solution)/shard_map/ppermute | solution.py:38
  72.4 14.8 %collective-permute-start.11 = (bf16[64,3072]{1,0:T(8,128)(2,1)S(1)}, bf16[64,3072]{1,0:T(8,128)(2,1)S(1)}, u32[]{:S(2)}, u32[]{:S(2)}) collective-permute-start(bf16[64,3072]{1,0:T(8,128)(2,1)S(1)} %add_convert_fusion.1), channel_id=1, source_target_pairs={{2,0},{6,1},{0,2},{4,3},{7,4},{3,5},{5,6},{1,7},{10,8},{14,9},{8,1... | collective-permute-start | bytes 1179656 | tf_op jit(solution)/shard_map/ppermute | solution.py:38

commit v2 on v1

v2 whole, which is shorter than its diff:
```python
import functools
import math

import jax
import jax.numpy as jnp
from jax import lax
from jax.experimental import pallas as pl
from jax.experimental.pallas import tpu as pltpu
from jax.sharding import PartitionSpec as P

EPSILON = 1e-06
CHIPS = 4
CORES = 2


def place(chip, core):
    return (chip % CHIPS) * CORES + core


NEAR_A = [
    (place(0, 0), place(1, 0)), (place(0, 1), place(3, 0)), (place(1, 0), place(0, 0)), (place(1, 1), place(2, 0)),
    (place(2, 0), place(3, 1)), (place(2, 1), place(1, 1)), (place(3, 0), place(2, 1)), (place(3, 1), place(0, 1)),
]
NEAR_B = [
    (place(0, 0), place(3, 0)), (place(0, 1), place(1, 0)), (place(1, 0), place(2, 0)), (place(1, 1), place(0, 0)),
    (place(2, 0), place(1, 1)), (place(2, 1), place(3, 1)), (place(3, 0), place(0, 1)), (place(3, 1), place(2, 1)),
]
SAME = [(place(0, 1), place(0, 0)), (place(1, 1), place(1, 0)), (place(2, 0), place(2, 1)), (place(3, 0), place(3, 1))]
FAR_A = [(place(1, 0), place(2, 0)), (place(0, 0), place(3, 0)), (place(3, 1), place(0, 1)), (place(2, 1), place(1, 1))]
FAR_B = [(place(3, 0), place(2, 0)), (place(2, 0), place(3, 0)), (place(1, 1), place(0, 1)), (place(0, 1), place(1, 1))]
SWAP = [(i, i ^ 1) for i in range(CHIPS * CORES)]
LOCAL = (place(0, 0), place(1, 0), place(2, 1), place(3, 1))


def back(pairs):
    return [(target, source) for source, target in pairs]


def send(value, pairs):
    return lax.ppermute(value, "mp", pairs)


def normalize(entries, gain):
    average = jnp.mean(entries, axis=-1, keepdims=True)
    centred = entries - average
    spread = jnp.mean(centred * centred, axis=-1, keepdims=True)
    return centred * lax.rsqrt(spread + EPSILON) * gain


def norm_rows(ref, gain_ref, normed, at):
    entries = ref[...].astype(jnp.float32)
    normed[at : at + ref.shape[0], :] = normalize(entries, gain_ref[...]).astype(jnp.bfloat16)


def normalize_heads(entries, gains, head_size):
    return jnp.concatenate(
        [
            normalize(entries[:, head * head_size : (head + 1) * head_size], gains[head : head + 1, :])
            for head in range(gains.shape[0])
        ],
        axis=1,
    ).astype(jnp.bfloat16)


def project_rows(rows, w_ref, qk_ref, at):
    heads, head_size = qk_ref.shape[1:]
    size = heads * head_size
    columns = slice(at, at + size)
    entries = jnp.dot(rows, w_ref[...], preferred_element_type=jnp.float32)
    return (
        columns,
        normalize_heads(entries[:, :size], qk_ref[0], head_size),
        normalize_heads(entries[:, size : 2 * size], qk_ref[1], head_size),
        entries[:, 2 * size :].astype(jnp.bfloat16),
    )


def attend(queries, keys, values, at, head_size, joined):
    for start in range(at, at + queries.shape[1] // 2, head_size):
        columns = slice(start, start + head_size)
        stacked = lambda refs: jnp.concatenate([ref[:, columns] for ref in refs], axis=0)
        scores = lax.dot_general(
            queries[:, columns], stacked(keys), (((1,), (1,)), ((), ())), preferred_element_type=jnp.float32
        ) * (1.0 / math.sqrt(head_size))
        raised = jnp.exp(scores - jnp.max(scores, axis=-1, keepdims=True))
        weights = (raised * (1.0 / jnp.sum(raised, axis=-1, keepdims=True))).astype(jnp.bfloat16)
        joined[:, columns] = jnp.dot(weights, stacked(values), preferred_element_type=jnp.float32).astype(jnp.bfloat16)


def out_terms(joined, w_ref, w2_ref, upper_ref, lower_ref):
    half, block = w_ref.shape[0], upper_ref.shape[0]
    for start in range(0, upper_ref.shape[1], 512):
        columns = slice(start, start + 512)
        term = jnp.dot(joined[:, :half], w_ref[:, columns], preferred_element_type=jnp.float32) + jnp.dot(
            joined[:, half:], w2_ref[:, columns], preferred_element_type=jnp.float32
        )
        upper_ref[:, columns] = term[:block].astype(jnp.bfloat16)
        lower_ref[:, columns] = term[block:].astype(jnp.bfloat16)


def first_kernel(a_ref, gain_ref, w_hbm, wo_hbm, normed, w_ref, wo_ref, sems):
    loads = [
        pltpu.make_async_copy(source, target, sems.at[i])
        for i, (source, target) in enumerate(((w_hbm, w_ref), (wo_hbm, wo_ref)))
    ]
    for load in loads:
        load.start()
    norm_rows(a_ref, gain_ref, normed, 0)
    for load in loads:
        load.wait()


def early_kernel(
    local_ref, own_ref, b_ref, same_ref, gain_ref, qk_ref, qk2_ref, w_ref, w2_ref, wo_ref, wo2_ref, near_ref,
    second_ref, third_ref, queries, near_keys, near_values, keys, values, normed, early, joined,
):
    block = own_ref.shape[0]
    heads, head_size = qk_ref.shape[1:]
    half = heads * head_size
    normed[:block, :] = near_ref[...]
    norm_rows(b_ref, gain_ref, normed, block)

    @pl.when(local_ref[0] == 1)
    def _():
        norm_rows(same_ref, gain_ref, normed, 2 * block)
        norm_rows(own_ref, gain_ref, normed, 3 * block)
        for at, qk, w in ((0, qk_ref, w_ref), (half, qk2_ref, w2_ref)):
            columns, some_queries, some_keys, some_values = project_rows(normed[...], w, qk, at)
            early[:, columns] = some_queries[block : 3 * block]
            queries[:block, columns] = some_queries[:block]
            queries[block:, columns] = some_queries[3 * block :]
            near_keys[:, columns] = some_keys[: 2 * block]
            keys[:, columns] = some_keys[2 * block :]
            near_values[:, columns] = some_values[: 2 * block]
            values[:, columns] = some_values[2 * block :]
            attend(early, (near_keys, keys), (near_values, values), at, head_size, joined)
        out_terms(joined, wo_ref, wo2_ref, second_ref, third_ref)

    @pl.when(local_ref[0] == 0)
    def _():
        for at, qk, w in ((0, qk_ref, w_ref), (half, qk2_ref, w2_ref)):
            columns, some_queries, some_keys, some_values = project_rows(normed[: 2 * block, :], w, qk, at)
            queries[:, columns] = some_queries
            near_keys[:, columns] = some_keys
            near_values[:, columns] = some_values


def far_kernel(
    local_ref, far_a_ref, far_b_ref, gain_ref, qk_ref, qk2_ref, w_ref, w2_ref, wo_ref, wo2_ref, near_keys, near_values,
    early_keys, early_values, third_ref, fourth_ref, keys, values, normed, queries, joined,
):
    block = far_a_ref.shape[0]
    heads, head_size = qk_ref.shape[1:]
    half = heads * head_size

    @pl.when(local_ref[0] == 1)
    def _():
        keys[...] = early_keys[...]
        values[...] = early_values[...]

    @pl.when(local_ref[0] == 0)
    def _():
        norm_rows(far_a_ref, gain_ref, normed, 0)
        norm_rows(far_b_ref, gain_ref, normed, block)
        for at, qk, w in ((0, qk_ref, w_ref), (half, qk2_ref, w2_ref)):
            columns, some_queries, some_keys, some_values = project_rows(normed[...], w, qk, at)
            queries[:, columns] = some_queries
            keys[:, columns] = some_keys
            values[:, columns] = some_values
            attend(queries, (near_keys, keys), (near_values, values), at, head_size, joined)
        out_terms(joined, wo_ref, wo2_ref, third_ref, fourth_ref)


def late_kernel(head_size, queries, near_keys, near_values, keys, values, wo_ref, wo2_ref, first_ref, other_ref, joined):
    half = wo_ref.shape[0]
    for at in (0, half):
        attend(queries, (near_keys, keys), (near_values, values), at, head_size, joined)
    out_terms(joined, wo_ref, wo2_ref, first_ref, other_ref)


def whole(count, space=pltpu.VMEM):
    return [pl.BlockSpec(memory_space=space)] * count


def held(value):
    return pltpu.with_memory_space_constraint(value, pltpu.VMEM)


def stored(value):
    return pltpu.with_memory_space_constraint(value, pltpu.HBM)


def body(tokens, ln_gain, w_in, qk_gain, w_out):
    block, width = tokens.shape
    heads, head_size = qk_gain.shape[1:]
    me = lax.axis_index("mp")
    local = (me // (CHIPS // 2 * CORES)) == (me % CORES)
    gain = ln_gain.reshape(1, width)

    near_a = send(tokens, NEAR_A)
    w_in2 = send(w_in, SWAP)
    w_out2 = send(w_out, SWAP)
    qk_gain2 = send(qk_gain, SWAP)
    same = send(tokens, SAME)
    near_b = send(tokens, NEAR_B)
    far_a = send(lax.optimization_barrier((near_a, same))[0], FAR_A)
    far_b = send(near_a, FAR_B)

    row_block = pltpu.VMEM((block, width), jnp.bfloat16)
    w2_vmem, wo2_vmem = held(w_in2), held(w_out2)
    normed, w_vmem, wo_vmem = pl.pallas_call(
        first_kernel,
        out_shape=(row_block, pltpu.VMEM(w_in.shape, jnp.bfloat16), pltpu.VMEM(w_out.shape, jnp.bfloat16)),
        in_specs=whole(2) + whole(2, pl.ANY),
        out_specs=tuple(whole(3)),
        scratch_shapes=[pltpu.SemaphoreType.DMA((2,))],
        compiler_params=pltpu.CompilerParams(vmem_limit_bytes=4 * 1024 * 1024),
        cost_estimate=pl.CostEstimate(flops=100000000000, bytes_accessed=10_000_000, transcendentals=0),
    )(held(near_a), gain, stored(w_in), stored(w_out))
    w_vmem, wo_vmem = held(w_vmem), held(wo_vmem)
    half_rows = pltpu.VMEM((2 * block, 2 * heads * head_size), jnp.bfloat16)
    half_normed = pltpu.VMEM((2 * block, width), jnp.bfloat16)
    flag = local.astype(jnp.int32).reshape(1)
    second, third, queries, near_keys, near_values, keys, values = pl.pallas_call(
        early_kernel,
        out_shape=(row_block, row_block) + (half_rows,) * 5,
        in_specs=whole(1, pltpu.SMEM) + whole(11),
        out_specs=tuple(whole(7)),
        scratch_shapes=[pltpu.VMEM((4 * block, width), jnp.bfloat16), half_rows, half_rows],
        compiler_params=pltpu.CompilerParams(vmem_limit_bytes=16 * 1024 * 1024),
        cost_estimate=pl.CostEstimate(flops=4_000_000_000, bytes_accessed=8_000_000, transcendentals=200_000),
    )(
        flag, held(tokens), held(near_b), held(same), gain, qk_gain, qk_gain2, w_vmem, w2_vmem, wo_vmem, wo2_vmem,
        held(normed),
    )
    to_near_b_early = send(second, [pair for pair in back(NEAR_B) if pair[0] in LOCAL])
    to_same = send(third, back(SAME))
    near_keys, near_values = held(near_keys), held(near_values)
    third, fourth, keys, values = pl.pallas_call(
        far_kernel,
        out_shape=(row_block, row_block, half_rows, half_rows),
        in_specs=whole(1, pltpu.SMEM) + whole(13),
        out_specs=tuple(whole(4)),
        scratch_shapes=[half_normed, half_rows, half_rows],
        compiler_params=pltpu.CompilerParams(vmem_limit_bytes=16 * 1024 * 1024),
        cost_estimate=pl.CostEstimate(flops=3_000_000_000, bytes_accessed=1_000_000, transcendentals=200_000),
    )(
        flag, held(far_a), held(far_b), gain, qk_gain, qk_gain2, w_vmem, w2_vmem, wo_vmem, wo2_vmem, near_keys,
        near_values, held(keys), held(values),
    )
    to_far_a = send(third, back(FAR_A))
    to_far_b = send(fourth, back(FAR_B))
    queries, to_near_b_early, to_same = lax.optimization_barrier((queries, to_near_b_early, to_same))
    first, other = pl.pallas_call(
        functools.partial(late_kernel, head_size),
        out_shape=(row_block, row_block),
        in_specs=whole(7),
        out_specs=tuple(whole(2)),
        scratch_shapes=[half_rows],
        compiler_params=pltpu.CompilerParams(vmem_limit_bytes=8 * 1024 * 1024),
        cost_estimate=pl.CostEstimate(flops=1_000_000_000, bytes_accessed=1_000_000, transcendentals=200_000),
    )(held(queries), near_keys, near_values, held(keys), held(values), wo_vmem, wo2_vmem)
    to_near_b = send(other, [pair for pair in back(NEAR_B) if pair[0] not in LOCAL])
    wide = lambda value: value.astype(jnp.float32)
    passed = (wide(first) + wide(jnp.where(local, to_far_a, to_far_b))).astype(jnp.bfloat16)
    to_near_a = send(passed, back(NEAR_A))
    kept = wide(tokens) + wide(jnp.where(local, other, to_same)) + wide(to_near_b) + wide(to_near_b_early)
    return (kept + wide(to_near_a)).astype(jnp.bfloat16)


def solution(mesh):
    return jax.shard_map(
        body,
        mesh=mesh,
        in_specs=(P(("dp", "mp"), None), P(), P(None, "mp"), P(None, "mp", None), P("mp", None)),
        out_specs=P(("dp", "mp"), None),
        check_vma=False,
    )
```

time: 88.7 us -> 80.8 us (0.911)
  the two profiles are of different devices: /device:TPU:699 before, /device:TPU:17 now
where the time goes in v2:
time: 80.8 us; the launch traced here: 80.3 us
  starting transfers between devices  46 us (57%)
  waiting for transfers between devices  18.2 us (23%)
  Pallas kernels  13.2 us (16%)
  local copies, waits for them, and re-layouts  1.4 us (2%)
  other arithmetic  1.23 us (2%)
    ppermute x14, starting transfers between devices, send(): return lax.ppermute(value, 'mp', pairs)  46 us
    ppermute x14, waiting for transfers between devices, send(): return lax.ppermute(value, 'mp', pairs)  18.2 us
    pallas_call x1, Pallas kernels, body(): pl.pallas_call(far_kernel, out_shape=(row_block, row_block, half_rows, ha...  4.8 us
    pallas_call x1, Pallas kernels, body(): pl.pallas_call(first_kernel, out_shape=(row_block, pltpu.VMEM(w_in.shape,...  3.75 us
    pallas_call x1, Pallas kernels, body(): pl.pallas_call(early_kernel, out_shape=(row_block, row_block) + (half_row...  2.69 us
    pallas_call x1, Pallas kernels, body(): pl.pallas_call(functools.partial(late_kernel, head_size), out_shape=(row_...  2 us
  transfers between devices with their start and end apart: 14, of which 4 were waited for; matrix products, arithmetic and copies ran while one was open for 1% of the time, Pallas kernels for 16%

profile of v2, /device:TPU:17, one launch (start us, length us, event | category | flops | bytes accessed | tf_op | source)
XLA Modules:
  0.0 80.3 jit_solution(5475659097683863468)
XLA Ops:
  0.0 2.6 %collective-permute-start.1 = (bf16[64,3072]{1,0:T(8,128)(2,1)}, bf16[64,3072]{1,0:T(8,128)(2,1)S(1)}, u32[]{:S(2)}, u32[]{:S(2)}) collective-permute-start(bf16[64,3072]{1,0:T(8,128)(2,1)} %own_ref.1), channel_id=1, source_target_pairs={{1,0},{3,2},{4,5},{6,7},{9,8},{11,10},{12,13},{14,15},{17,16},{19,... | collective-permute-start | bytes 1179656 | tf_op jit(solution)/shard_map/ppermute | solution.py:40
  2.6 5.2 %collective-permute-start.3 = (bf16[64,3072]{1,0:T(8,128)(2,1)}, bf16[64,3072]{1,0:T(8,128)(2,1)S(1)}, u32[]{:S(2)}, u32[]{:S(2)}) collective-permute-start(bf16[64,3072]{1,0:T(8,128)(2,1)} %own_ref.1), channel_id=1, source_target_pairs={{0,2},{1,6},{2,0},{3,4},{4,7},{5,3},{6,5},{7,1},{8,10},{9,14},{10,... | collective-permute-start | bytes 1179656 | tf_op jit(solution)/shard_map/ppermute | solution.py:40
  7.8 0.7 copy.7.qk_ref
  8.4 7.4 %collective-permute-start.2 = (f32[2,3,128]{2,1,0:T(4,128)S(1)}, f32[2,3,128]{2,1,0:T(4,128)S(1)}, u32[]{:S(2)}, u32[]{:S(2)}) collective-permute-start(f32[2,3,128]{2,1,0:T(4,128)S(1)} %copy.7.qk_ref), channel_id=1, source_target_pairs={{0,1},{1,0},{2,3},{3,2},{4,5},{5,4},{6,7},{7,6},{8,9},{9,8},{10,11... | collective-permute-start | bytes 9224 | tf_op jit(solution)/shard_map/ppermute | solution.py:40
  15.8 2.7 %collective-permute-start = (bf16[64,3072]{1,0:T(8,128)(2,1)}, bf16[64,3072]{1,0:T(8,128)(2,1)S(1)}, u32[]{:S(2)}, u32[]{:S(2)}) collective-permute-start(bf16[64,3072]{1,0:T(8,128)(2,1)} %own_ref.1), channel_id=1, source_target_pairs={{0,6},{1,2},{2,4},{3,0},{4,3},{5,7},{6,1},{7,5},{8,14},{9,10},{10,... | collective-permute-start | bytes 1179656 | tf_op jit(solution)/shard_map/ppermute | solution.py:40
  18.5 1.9 %collective-permute-start.5 = (bf16[384,3072]{1,0:T(8,128)(2,1)}, bf16[384,3072]{1,0:T(8,128)(2,1)S(1)}, u32[]{:S(2)}, u32[]{:S(2)}) collective-permute-start(bf16[384,3072]{1,0:T(8,128)(2,1)} %wo_hbm.1), channel_id=1, source_target_pairs={{0,1},{1,0},{2,3},{3,2},{4,5},{5,4},{6,7},{7,6},{8,9},{9,8},{10,11... | collective-permute-start | bytes 7077896 | tf_op jit(solution)/shard_map/ppermute | solution.py:40
  20.5 0.0 collective-permute-done.1.same_ref
  20.5 2.4 %collective-permute-start.4 = (bf16[3072,1152]{1,0:T(8,128)(2,1)}, bf16[3072,1152]{1,0:T(8,128)(2,1)S(1)}, u32[]{:S(2)}, u32[]{:S(2)}) collective-permute-start(bf16[3072,1152]{1,0:T(8,128)(2,1)} %w_hbm.1), channel_id=1, source_target_pairs={{0,1},{1,0},{2,3},{3,2},{4,5},{5,4},{6,7},{7,6},{8,9},{9,8},{10,11... | collective-permute-start | bytes 21233672 | tf_op jit(solution)/shard_map/ppermute | solution.py:40
  22.9 0.0 collective-permute-done.3.a_ref
  22.9 1.3 %collective-permute-start.8 = (bf16[64,3072]{1,0:T(8,128)(2,1)S(1)}, bf16[64,3072]{1,0:T(8,128)(2,1)S(1)}, u32[]{:S(2)}, u32[]{:S(2)}) collective-permute-start(bf16[64,3072]{1,0:T(8,128)(2,1)S(1)} %collective-permute-done.3.a_ref), channel_id=1, source_target_pairs={{2,4},{0,6},{7,1},{5,3},{10,12},{8,14},{15,9},{13,11},{18,20},{16,... | collective-permute-start | bytes 1179656 | tf_op jit(solution)/shard_map/ppermute | solution.py:40
  24.2 0.0 collective-permute-done.2.qk2_ref
  24.2 8.1 %collective-permute-start.9 = (bf16[64,3072]{1,0:T(8,128)(2,1)S(1)}, bf16[64,3072]{1,0:T(8,128)(2,1)S(1)}, u32[]{:S(2)}, u32[]{:S(2)}) collective-permute-start(bf16[64,3072]{1,0:T(8,128)(2,1)S(1)} %collective-permute-done.3.a_ref), channel_id=1, source_target_pairs={{6,4},{4,6},{3,1},{1,3},{14,12},{12,14},{11,9},{9,11},{22,20},{20,... | collective-permute-start | bytes 1179656 | tf_op jit(solution)/shard_map/ppermute | solution.py:40
  32.3 0.0 copy-start.1
  32.3 0.7 copy-done.1
  33.0 0.0 copy-start
  33.0 0.0 copy-start.2
  33.0 3.7 %shard_map.55 = (bf16[64,3072]{1,0:T(8,128)(2,1)S(1)}, bf16[3072,1152]{1,0:T(8,128)(2,1)S(1)}, bf16[384,3072]{1,0:T(8,128)(2,1)S(1)}) custom-call(bf16[64,3072]{1,0:T(8,128)(2,1)S(1)} %collective-permute-done.3.a_ref, f32[1,3072]{1,0:T(1,128)S(1)} %bitcast.2, bf16[3072,1152]{1,0:T(8,128)(2,1)} %w_hbm.1, bf16[384,3072]{1,0:T(8,128)(2,1)} %wo_hbm.1), custom_call_target="tpu_custom_call" | custom-call | flops 99999997952 | bytes 10000000 | tf_op jit(solution)/shard_map/pallas_call | solution.py:211
  36.8 0.0 collective-permute-done.b_ref
  36.8 0.0 collective-permute-done.5.wo2_ref
  36.8 0.0 collective-permute-done.4.w2_ref
  36.8 0.0 copy-done
  36.8 0.0 copy-done.2
  36.8 2.7 %shard_map.56 = (bf16[64,3072]{1,0:T(8,128)(2,1)S(1)}, bf16[64,3072]{1,0:T(8,128)(2,1)S(1)}, bf16[128,768]{1,0:T(8,128)(2,1)S(1)}, bf16[128,768]{1,0:T(8,128)(2,...) custom-call(s32[1]{0:T(128)} %bitcast.local_ref, ...), custom_call_target="tpu_custom_call" | custom-call | flops 4000000000 | bytes 8000000 | tf_op jit(solution)/shard_map/pallas_call | solution.py:224
  39.5 1.3 %collective-permute-start.6 = (bf16[64,3072]{1,0:T(8,128)(2,1)S(1)}, bf16[64,3072]{1,0:T(8,128)(2,1)S(1)}, u32[]{:S(2)}, u32[]{:S(2)}) collective-permute-start(bf16[64,3072]{1,0:T(8,128)(2,1)S(1)} %get-tuple-element.29), channel_id=1, source_target_pairs={{2,1},{0,3},{7,5},{5,7},{10,9},{8,11},{15,13},{13,15},{18,17},{16,... | collective-permute-start | bytes 1179656 | tf_op jit(solution)/shard_map/ppermute | solution.py:40
  40.8 1.3 %collective-permute-start.7 = (bf16[64,3072]{1,0:T(8,128)(2,1)S(1)}, bf16[64,3072]{1,0:T(8,128)(2,1)S(1)}, u32[]{:S(2)}, u32[]{:S(2)}) collective-permute-start(bf16[64,3072]{1,0:T(8,128)(2,1)S(1)} %get-tuple-element.30), channel_id=1, source_target_pairs={{0,1},{2,3},{5,4},{7,6},{8,9},{10,11},{13,12},{15,14},{16,17},{18,... | collective-permute-start | bytes 1179656 | tf_op jit(solution)/shard_map/ppermute | solution.py:40
  42.1 0.0 collective-permute-done.8.far_a_ref
  42.2 0.0 collective-permute-done.9.far_b_ref
  42.2 4.8 %shard_map.57 = (bf16[64,3072]{1,0:T(8,128)(2,1)S(1)}, bf16[64,3072]{1,0:T(8,128)(2,1)S(1)}, bf16[128,768]{1,0:T(8,128)(2,1)S(1)}, bf16[128,768]{1,0:T(8,128)(2,1)S(1)}) custom-call(s32[1]{0:T(128)} %bitcast.local_ref, bf16[64,3072]{1,0:T(8,128)(2,1)S(1)} %collective-permute-done.8.far_a_ref, bf16[64,3072]{1,0:T(8,128)(2,1)S(1)} %collective-permute-done.9.far_b_ref, ...), custom_call_target="tpu_custom_call" | custom-call | flops 3000000000 | bytes 1000000 | tf_op jit(solution)/shard_map/pallas_call | solution.py:239
  47.0 5.0 %collective-permute-start.11 = (bf16[64,3072]{1,0:T(8,128)(2,1)S(1)}, bf16[64,3072]{1,0:T(8,128)(2,1)S(1)}, u32[]{:S(2)}, u32[]{:S(2)}) collective-permute-start(bf16[64,3072]{1,0:T(8,128)(2,1)S(1)} %get-tuple-element.43), channel_id=1, source_target_pairs={{4,2},{6,0},{1,7},{3,5},{12,10},{14,8},{9,15},{11,13},{20,18},{22,... | collective-permute-start | bytes 1179656 | tf_op jit(solution)/shard_map/ppermute | solution.py:40
  52.0 2.9 %collective-permute-start.12 = (bf16[64,3072]{1,0:T(8,128)(2,1)S(1)}, bf16[64,3072]{1,0:T(8,128)(2,1)S(1)}, u32[]{:S(2)}, u32[]{:S(2)}) collective-permute-start(bf16[64,3072]{1,0:T(8,128)(2,1)S(1)} %get-tuple-element.44), channel_id=1, source_target_pairs={{4,6},{6,4},{1,3},{3,1},{12,14},{14,12},{9,11},{11,9},{20,22},{22,... | collective-permute-start | bytes 1179656 | tf_op jit(solution)/shard_map/ppermute | solution.py:40
  54.9 1.7 %collective-permute-done.6 = bf16[64,3072]{1,0:T(8,128)(2,1)S(1)} collective-permute-done((bf16[64,3072]{1,0:T(8,128)(2,1)S(1)}, bf16[64,3072]{1,0:T(8,128)(2,1)S(1)}, u32[]{:S(2)}, u32[]{:S(2)}) %collective-permute-start.6) | collective-permute-done | bytes 393248 | tf_op jit(solution)/shard_map/ppermute | solution.py:40
  56.6 0.0 collective-permute-done.7
  56.6 2.0 %shard_map.58 = (bf16[64,3072]{1,0:T(8,128)(2,1)S(1)}, bf16[64,3072]{1,0:T(8,128)(2,1)S(1)}) custom-call(bf16[128,768]{1,0:T(8,128)(2,1)S(1)} %get-tuple-element.31.queries, bf16[128,768]{1,0:T(8,128)(2,1)S(1)} %get-tuple-element.32.near_keys, bf16[128,768]{1,0:T(8,128)(2,1)S(1)} %get-tuple-element.33.near_values, ...), custom_call_target="tpu_custom_call" | custom-call | flops 1000000000 | bytes 1000000 | tf_op jit(solution)/shard_map/pallas_call | solution.py:254
  58.6 2.0 %collective-permute-start.10 = (bf16[64,3072]{1,0:T(8,128)(2,1)S(1)}, bf16[64,3072]{1,0:T(8,128)(2,1)S(1)}, u32[]{:S(2)}, u32[]{:S(2)}) collective-permute-start(bf16[64,3072]{1,0:T(8,128)(2,1)S(1)} %get-tuple-element.39), channel_id=1, source_target_pairs={{6,0},{4,2},{3,4},{1,6},{14,8},{12,10},{11,12},{9,14},{22,16},{20,... | collective-permute-start | bytes 1179656 | tf_op jit(solution)/shard_map/ppermute | solution.py:40
  60.7 0.0 collective-permute-done.11
  60.7 4.8 %collective-permute-done.12 = bf16[64,3072]{1,0:T(8,128)(2,1)S(1)} collective-permute-done((bf16[64,3072]{1,0:T(8,128)(2,1)S(1)}, bf16[64,3072]{1,0:T(8,128)(2,1)S(1)}, u32[]{:S(2)}, u32[]{:S(2)}) %collective-permute-start.12) | collective-permute-done | bytes 393248 | tf_op jit(solution)/shard_map/ppermute | solution.py:40
  65.5 0.1 add_convert_fusion.1
  65.7 1.9 %collective-permute-start.13 = (bf16[64,3072]{1,0:T(8,128)(2,1)S(1)}, bf16[64,3072]{1,0:T(8,128)(2,1)S(1)}, u32[]{:S(2)}, u32[]{:S(2)}) collective-permute-start(bf16[64,3072]{1,0:T(8,128)(2,1)S(1)} %add_convert_fusion.1), channel_id=1, source_target_pairs={{2,0},{6,1},{0,2},{4,3},{7,4},{3,5},{5,6},{1,7},{10,8},{14,9},{8,1... | collective-permute-start | bytes 1179656 | tf_op jit(solution)/shard_map/ppermute | solution.py:40
  67.6 0.7 collective-permute-done.10
  68.3 10.9 %collective-permute-done.13 = bf16[64,3072]{1,0:T(8,128)(2,1)S(1)} collective-permute-done((bf16[64,3072]{1,0:T(8,128)(2,1)S(1)}, bf16[64,3072]{1,0:T(8,128)(2,1)S(1)}, u32[]{:S(2)}, u32[]{:S(2)}) %collective-permute-start.13) | collective-permute-done | bytes 393248 | tf_op jit(solution)/shard_map/ppermute | solution.py:40
  79.2 1.1 %add_convert_fusion = bf16[64,3072]{1,0:T(8,128)(2,1)} fusion(bf16[64,3072]{1,0:T(8,128)(2,1)S(1)} %collective-permute-done.13, bf16[64,3072]{1,0:T(8,128)(2,1)S(1)} %collective-permute-done.6, bf16[64,3072]{1,0:T(8,128)(2,1)S(1)} %collective-permute-done.10, bf16[64,3072]{1,0:T(8,128)(2,1)S(1)} %copy-done, bf16[64,3072]{1,0:T(8,128)(2,1)S(1)} %get-tuple-element.39, ...), kind=kLoop, calls=%fused_computation | loop fusion | flops 2162688 | bytes 2752513 | tf_op jit(solution)/shard_map/convert_element_type | solution.py:268
Async XLA Ops:
  0.0 20.5 %collective-permute-start.1 = (bf16[64,3072]{1,0:T(8,128)(2,1)}, bf16[64,3072]{1,0:T(8,128)(2,1)S(1)}, u32[]{:S(2)}, u32[]{:S(2)}) collective-permute-start(bf16[64,3072]{1,0:T(8,128)(2,1)} %own_ref.1), channel_id=1, source_target_pairs={{1,0},{3,2},{4,5},{6,7},{9,8},{11,10},{12,13},{14,15},{17,16},{19,... | collective-permute-start | bytes 1179656 | tf_op jit(solution)/shard_map/ppermute | solution.py:40
  2.6 20.3 %collective-permute-start.3 = (bf16[64,3072]{1,0:T(8,128)(2,1)}, bf16[64,3072]{1,0:T(8,128)(2,1)S(1)}, u32[]{:S(2)}, u32[]{:S(2)}) collective-permute-start(bf16[64,3072]{1,0:T(8,128)(2,1)} %own_ref.1), channel_id=1, source_target_pairs={{0,2},{1,6},{2,0},{3,4},{4,7},{5,3},{6,5},{7,1},{8,10},{9,14},{10,... | collective-permute-start | bytes 1179656 | tf_op jit(solution)/shard_map/ppermute | solution.py:40
  8.4 15.8 %collective-permute-start.2 = (f32[2,3,128]{2,1,0:T(4,128)S(1)}, f32[2,3,128]{2,1,0:T(4,128)S(1)}, u32[]{:S(2)}, u32[]{:S(2)}) collective-permute-start(f32[2,3,128]{2,1,0:T(4,128)S(1)} %copy.7.qk_ref), channel_id=1, source_target_pairs={{0,1},{1,0},{2,3},{3,2},{4,5},{5,4},{6,7},{7,6},{8,9},{9,8},{10,11... | collective-permute-start | bytes 9224 | tf_op jit(solution)/shard_map/ppermute | solution.py:40
  15.8 21.0 %collective-permute-start = (bf16[64,3072]{1,0:T(8,128)(2,1)}, bf16[64,3072]{1,0:T(8,128)(2,1)S(1)}, u32[]{:S(2)}, u32[]{:S(2)}) collective-permute-start(bf16[64,3072]{1,0:T(8,128)(2,1)} %own_ref.1), channel_id=1, source_target_pairs={{0,6},{1,2},{2,4},{3,0},{4,3},{5,7},{6,1},{7,5},{8,14},{9,10},{10,... | collective-permute-start | bytes 1179656 | tf_op jit(solution)/shard_map/ppermute | solution.py:40
  18.5 18.3 %collective-permute-start.5 = (bf16[384,3072]{1,0:T(8,128)(2,1)}, bf16[384,3072]{1,0:T(8,128)(2,1)S(1)}, u32[]{:S(2)}, u32[]{:S(2)}) collective-permute-start(bf16[384,3072]{1,0:T(8,128)(2,1)} %wo_hbm.1), channel_id=1, source_target_pairs={{0,1},{1,0},{2,3},{3,2},{4,5},{5,4},{6,7},{7,6},{8,9},{9,8},{10,11... | collective-permute-start | bytes 7077896 | tf_op jit(solution)/shard_map/ppermute | solution.py:40
  20.5 16.3 %collective-permute-start.4 = (bf16[3072,1152]{1,0:T(8,128)(2,1)}, bf16[3072,1152]{1,0:T(8,128)(2,1)S(1)}, u32[]{:S(2)}, u32[]{:S(2)}) collective-permute-start(bf16[3072,1152]{1,0:T(8,128)(2,1)} %w_hbm.1), channel_id=1, source_target_pairs={{0,1},{1,0},{2,3},{3,2},{4,5},{5,4},{6,7},{7,6},{8,9},{9,8},{10,11... | collective-permute-start | bytes 21233672 | tf_op jit(solution)/shard_map/ppermute | solution.py:40
  22.9 19.3 %collective-permute-start.8 = (bf16[64,3072]{1,0:T(8,128)(2,1)S(1)}, bf16[64,3072]{1,0:T(8,128)(2,1)S(1)}, u32[]{:S(2)}, u32[]{:S(2)}) collective-permute-start(bf16[64,3072]{1,0:T(8,128)(2,1)S(1)} %collective-permute-done.3.a_ref), channel_id=1, source_target_pairs={{2,4},{0,6},{7,1},{5,3},{10,12},{8,14},{15,9},{13,11},{18,20},{16,... | collective-permute-start | bytes 1179656 | tf_op jit(solution)/shard_map/ppermute | solution.py:40
  24.2 18.0 %collective-permute-start.9 = (bf16[64,3072]{1,0:T(8,128)(2,1)S(1)}, bf16[64,3072]{1,0:T(8,128)(2,1)S(1)}, u32[]{:S(2)}, u32[]{:S(2)}) collective-permute-start(bf16[64,3072]{1,0:T(8,128)(2,1)S(1)} %collective-permute-done.3.a_ref), channel_id=1, source_target_pairs={{6,4},{4,6},{3,1},{1,3},{14,12},{12,14},{11,9},{9,11},{22,20},{20,... | collective-permute-start | bytes 1179656 | tf_op jit(solution)/shard_map/ppermute | solution.py:40
  32.3 0.7 copy-start.1
  33.0 3.8 %copy-start = (bf16[64,3072]{1,0:T(8,128)(2,1)S(1)}, bf16[64,3072]{1,0:T(8,128)(2,1)}, u32[]{:S(2)}) copy-start(bf16[64,3072]{1,0:T(8,128)(2,1)} %own_ref.1) | copy-start | bytes 1179652
  33.0 3.8 %copy-start.2 = (f32[3072]{0:T(1024)S(1)}, f32[3072]{0:T(1024)}, u32[]{:S(2)}) copy-start(f32[3072]{0:T(1024)} %param.6) | copy-start | bytes 36868
  39.5 17.1 %collective-permute-start.6 = (bf16[64,3072]{1,0:T(8,128)(2,1)S(1)}, bf16[64,3072]{1,0:T(8,128)(2,1)S(1)}, u32[]{:S(2)}, u32[]{:S(2)}) collective-permute-start(bf16[64,3072]{1,0:T(8,128)(2,1)S(1)} %get-tuple-element.29), channel_id=1, source_target_pairs={{2,1},{0,3},{7,5},{5,7},{10,9},{8,11},{15,13},{13,15},{18,17},{16,... | collective-permute-start | bytes 1179656 | tf_op jit(solution)/shard_map/ppermute | solution.py:40
  40.8 15.8 %collective-permute-start.7 = (bf16[64,3072]{1,0:T(8,128)(2,1)S(1)}, bf16[64,3072]{1,0:T(8,128)(2,1)S(1)}, u32[]{:S(2)}, u32[]{:S(2)}) collective-permute-start(bf16[64,3072]{1,0:T(8,128)(2,1)S(1)} %get-tuple-element.30), channel_id=1, source_target_pairs={{0,1},{2,3},{5,4},{7,6},{8,9},{10,11},{13,12},{15,14},{16,17},{18,... | collective-permute-start | bytes 1179656 | tf_op jit(solution)/shard_map/ppermute | solution.py:40
  47.0 13.7 %collective-permute-start.11 = (bf16[64,3072]{1,0:T(8,128)(2,1)S(1)}, bf16[64,3072]{1,0:T(8,128)(2,1)S(1)}, u32[]{:S(2)}, u32[]{:S(2)}) collective-permute-start(bf16[64,3072]{1,0:T(8,128)(2,1)S(1)} %get-tuple-element.43), channel_id=1, source_target_pairs={{4,2},{6,0},{1,7},{3,5},{12,10},{14,8},{9,15},{11,13},{20,18},{22,... | collective-permute-start | bytes 1179656 | tf_op jit(solution)/shard_map/ppermute | solution.py:40
  52.0 13.5 %collective-permute-start.12 = (bf16[64,3072]{1,0:T(8,128)(2,1)S(1)}, bf16[64,3072]{1,0:T(8,128)(2,1)S(1)}, u32[]{:S(2)}, u32[]{:S(2)}) collective-permute-start(bf16[64,3072]{1,0:T(8,128)(2,1)S(1)} %get-tuple-element.44), channel_id=1, source_target_pairs={{4,6},{6,4},{1,3},{3,1},{12,14},{14,12},{9,11},{11,9},{20,22},{22,... | collective-permute-start | bytes 1179656 | tf_op jit(solution)/shard_map/ppermute | solution.py:40
  58.6 9.6 %collective-permute-start.10 = (bf16[64,3072]{1,0:T(8,128)(2,1)S(1)}, bf16[64,3072]{1,0:T(8,128)(2,1)S(1)}, u32[]{:S(2)}, u32[]{:S(2)}) collective-permute-start(bf16[64,3072]{1,0:T(8,128)(2,1)S(1)} %get-tuple-element.39), channel_id=1, source_target_pairs={{6,0},{4,2},{3,4},{1,6},{14,8},{12,10},{11,12},{9,14},{22,16},{20,... | collective-permute-start | bytes 1179656 | tf_op jit(solution)/shard_map/ppermute | solution.py:40
  65.7 13.6 %collective-permute-start.13 = (bf16[64,3072]{1,0:T(8,128)(2,1)S(1)}, bf16[64,3072]{1,0:T(8,128)(2,1)S(1)}, u32[]{:S(2)}, u32[]{:S(2)}) collective-permute-start(bf16[64,3072]{1,0:T(8,128)(2,1)S(1)} %add_convert_fusion.1), channel_id=1, source_target_pairs={{2,0},{6,1},{0,2},{4,3},{7,4},{3,5},{5,6},{1,7},{10,8},{14,9},{8,1... | collective-permute-start | bytes 1179656 | tf_op jit(solution)/shard_map/ppermute | solution.py:40

commit v3 on v2

--- a/solution.py
+++ b/solution.py
@@ -98,14 +98,13 @@
         lower_ref[:, columns] = term[block:].astype(jnp.bfloat16)
 
 
-def first_kernel(a_ref, gain_ref, w_hbm, wo_hbm, normed, w_ref, wo_ref, sems):
+def first_kernel(a_ref, w_hbm, wo_hbm, w_ref, wo_ref, sems):
     loads = [
         pltpu.make_async_copy(source, target, sems.at[i])
         for i, (source, target) in enumerate(((w_hbm, w_ref), (wo_hbm, wo_ref)))
     ]
     for load in loads:
         load.start()
-    norm_rows(a_ref, gain_ref, normed, 0)
     for load in loads:
         load.wait()
 
@@ -117,7 +116,7 @@
     block = own_ref.shape[0]
     heads, head_size = qk_ref.shape[1:]
     half = heads * head_size
-    normed[:block, :] = near_ref[...]
+    norm_rows(near_ref, gain_ref, normed, 0)
     norm_rows(b_ref, gain_ref, normed, block)
 
     @pl.when(local_ref[0] == 1)
@@ -208,15 +207,15 @@
 
     row_block = pltpu.VMEM((block, width), jnp.bfloat16)
     w2_vmem, wo2_vmem = held(w_in2), held(w_out2)
-    normed, w_vmem, wo_vmem = pl.pallas_call(
+    w_vmem, wo_vmem = pl.pallas_call(
         first_kernel,
-        out_shape=(row_block, pltpu.VMEM(w_in.shape, jnp.bfloat16), pltpu.VMEM(w_out.shape, jnp.bfloat16)),
-        in_specs=whole(2) + whole(2, pl.ANY),
-        out_specs=tuple(whole(3)),
+        out_shape=(pltpu.VMEM(w_in.shape, jnp.bfloat16), pltpu.VMEM(w_out.shape, jnp.bfloat16)),
+        in_specs=whole(1) + whole(2, pl.ANY),
+        out_specs=tuple(whole(2)),
         scratch_shapes=[pltpu.SemaphoreType.DMA((2,))],
         compiler_params=pltpu.CompilerParams(vmem_limit_bytes=4 * 1024 * 1024),
         cost_estimate=pl.CostEstimate(flops=100000000000, bytes_accessed=10_000_000, transcendentals=0),
-    )(held(near_a), gain, stored(w_in), stored(w_out))
+    )(held(near_a), stored(w_in), stored(w_out))
     w_vmem, wo_vmem = held(w_vmem), held(wo_vmem)
     half_rows = pltpu.VMEM((2 * block, 2 * heads * head_size), jnp.bfloat16)
     half_normed = pltpu.VMEM((2 * block, width), jnp.bfloat16)
@@ -231,7 +230,7 @@
         cost_estimate=pl.CostEstimate(flops=4_000_000_000, bytes_accessed=8_000_000, transcendentals=200_000),
     )(
         flag, held(tokens), held(near_b), held(same), gain, qk_gain, qk_gain2, w_vmem, w2_vmem, wo_vmem, wo2_vmem,
-        held(normed),
+        held(near_a),
     )
     to_near_b_early = send(second, [pair for pair in back(NEAR_B) if pair[0] in LOCAL])
     to_same = send(third, back(SAME))
@@ -265,6 +264,7 @@
     passed = (wide(first) + wide(jnp.where(local, to_far_a, to_far_b))).astype(jnp.bfloat16)
     to_near_a = send(passed, back(NEAR_A))
     kept = wide(tokens) + wide(jnp.where(local, other, to_same)) + wide(to_near_b) + wide(to_near_b_early)
+    kept = lax.optimization_barrier(kept)
     return (kept + wide(to_near_a)).astype(jnp.bfloat16)
 
 

time: 80.8 us -> 81.3 us (level)
  no operation moved by 1% of the time
where the time goes in v3:
time: 81.3 us; the launch traced here: 80.9 us
  starting transfers between devices  46.7 us (57%)
  waiting for transfers between devices  18.6 us (23%)
  Pallas kernels  13.3 us (16%)
  other arithmetic  1.2 us (1%)
    ppermute x14, starting transfers between devices, send(): return lax.ppermute(value, 'mp', pairs)  46.7 us
    ppermute x14, waiting for transfers between devices, send(): return lax.ppermute(value, 'mp', pairs)  18.6 us
    pallas_call x1, Pallas kernels, body(): pl.pallas_call(far_kernel, out_shape=(row_block, row_block, half_rows, ha...  4.77 us
    pallas_call x1, Pallas kernels, body(): pl.pallas_call(first_kernel, out_shape=(pltpu.VMEM(w_in.shape, jnp.bfloat...  3.71 us
    pallas_call x1, Pallas kernels, body(): pl.pallas_call(early_kernel, out_shape=(row_block, row_block) + (half_row...  2.85 us
    pallas_call x1, Pallas kernels, body(): pl.pallas_call(functools.partial(late_kernel, head_size), out_shape=(row_...  2 us
  transfers between devices with their start and end apart: 14, of which 4 were waited for; matrix products, arithmetic and copies ran while one was open for 1% of the time, Pallas kernels for 16%

profile of v3, /device:TPU:17, one launch (start us, length us, event | category | flops | bytes accessed | tf_op | source)
XLA Modules:
  0.0 80.9 jit_solution(14978761921306386127)
XLA Ops:
  0.0 2.6 %collective-permute-start.1 = (bf16[64,3072]{1,0:T(8,128)(2,1)}, bf16[64,3072]{1,0:T(8,128)(2,1)S(1)}, u32[]{:S(2)}, u32[]{:S(2)}) collective-permute-start(bf16[64,3072]{1,0:T(8,128)(2,1)} %own_ref.1), channel_id=1, source_target_pairs={{1,0},{3,2},{4,5},{6,7},{9,8},{11,10},{12,13},{14,15},{17,16},{19,... | collective-permute-start | bytes 1179656 | tf_op jit(solution)/shard_map/ppermute | solution.py:40
  2.6 5.2 %collective-permute-start.3 = (bf16[64,3072]{1,0:T(8,128)(2,1)}, bf16[64,3072]{1,0:T(8,128)(2,1)S(1)}, u32[]{:S(2)}, u32[]{:S(2)}) collective-permute-start(bf16[64,3072]{1,0:T(8,128)(2,1)} %own_ref.1), channel_id=1, source_target_pairs={{0,2},{1,6},{2,0},{3,4},{4,7},{5,3},{6,5},{7,1},{8,10},{9,14},{10,... | collective-permute-start | bytes 1179656 | tf_op jit(solution)/shard_map/ppermute | solution.py:40
  7.8 0.7 copy.7.qk_ref
  8.4 7.4 %collective-permute-start.2 = (f32[2,3,128]{2,1,0:T(4,128)S(1)}, f32[2,3,128]{2,1,0:T(4,128)S(1)}, u32[]{:S(2)}, u32[]{:S(2)}) collective-permute-start(f32[2,3,128]{2,1,0:T(4,128)S(1)} %copy.7.qk_ref), channel_id=1, source_target_pairs={{0,1},{1,0},{2,3},{3,2},{4,5},{5,4},{6,7},{7,6},{8,9},{9,8},{10,11... | collective-permute-start | bytes 9224 | tf_op jit(solution)/shard_map/ppermute | solution.py:40
  15.8 2.7 %collective-permute-start = (bf16[64,3072]{1,0:T(8,128)(2,1)}, bf16[64,3072]{1,0:T(8,128)(2,1)S(1)}, u32[]{:S(2)}, u32[]{:S(2)}) collective-permute-start(bf16[64,3072]{1,0:T(8,128)(2,1)} %own_ref.1), channel_id=1, source_target_pairs={{0,6},{1,2},{2,4},{3,0},{4,3},{5,7},{6,1},{7,5},{8,14},{9,10},{10,... | collective-permute-start | bytes 1179656 | tf_op jit(solution)/shard_map/ppermute | solution.py:40
  18.5 1.9 %collective-permute-start.5 = (bf16[384,3072]{1,0:T(8,128)(2,1)}, bf16[384,3072]{1,0:T(8,128)(2,1)S(1)}, u32[]{:S(2)}, u32[]{:S(2)}) collective-permute-start(bf16[384,3072]{1,0:T(8,128)(2,1)} %wo_hbm.1), channel_id=1, source_target_pairs={{0,1},{1,0},{2,3},{3,2},{4,5},{5,4},{6,7},{7,6},{8,9},{9,8},{10,11... | collective-permute-start | bytes 7077896 | tf_op jit(solution)/shard_map/ppermute | solution.py:40
  20.5 0.0 copy-start
  20.5 0.0 copy-start.1
  20.5 0.0 collective-permute-done.1.same_ref
  20.5 2.5 %collective-permute-start.4 = (bf16[3072,1152]{1,0:T(8,128)(2,1)}, bf16[3072,1152]{1,0:T(8,128)(2,1)S(1)}, u32[]{:S(2)}, u32[]{:S(2)}) collective-permute-start(bf16[3072,1152]{1,0:T(8,128)(2,1)} %w_hbm.1), channel_id=1, source_target_pairs={{0,1},{1,0},{2,3},{3,2},{4,5},{5,4},{6,7},{7,6},{8,9},{9,8},{10,11... | collective-permute-start | bytes 21233672 | tf_op jit(solution)/shard_map/ppermute | solution.py:40
  23.0 0.0 collective-permute-done.3.a_ref.near_ref
  23.1 1.3 %collective-permute-start.8 = (bf16[64,3072]{1,0:T(8,128)(2,1)S(1)}, bf16[64,3072]{1,0:T(8,128)(2,1)S(1)}, u32[]{:S(2)}, u32[]{:S(2)}) collective-permute-start(bf16[64,3072]{1,0:T(8,128)(2,1)S(1)} %collective-permute-done.3.a_ref.near_ref), channel_id=1, source_target_pairs={{2,4},{0,6},{7,1},{5,3},{10,12},{8,14},{15,9},{13,11},{18,20},{16,... | collective-permute-start | bytes 1179656 | tf_op jit(solution)/shard_map/ppermute | solution.py:40
  24.4 0.0 collective-permute-done.2.qk2_ref
  24.4 8.0 %collective-permute-start.9 = (bf16[64,3072]{1,0:T(8,128)(2,1)S(1)}, bf16[64,3072]{1,0:T(8,128)(2,1)S(1)}, u32[]{:S(2)}, u32[]{:S(2)}) collective-permute-start(bf16[64,3072]{1,0:T(8,128)(2,1)S(1)} %collective-permute-done.3.a_ref.near_ref), channel_id=1, source_target_pairs={{6,4},{4,6},{3,1},{1,3},{14,12},{12,14},{11,9},{9,11},{22,20},{20,... | collective-permute-start | bytes 1179656 | tf_op jit(solution)/shard_map/ppermute | solution.py:40
  32.3 3.7 %shard_map.55 = (bf16[3072,1152]{1,0:T(8,128)(2,1)S(1)}, bf16[384,3072]{1,0:T(8,128)(2,1)S(1)}) custom-call(bf16[64,3072]{1,0:T(8,128)(2,1)S(1)} %collective-permute-done.3.a_ref.near_ref, bf16[3072,1152]{1,0:T(8,128)(2,1)} %w_hbm.1, bf16[384,3072]{1,0:T(8,128)(2,1)} %wo_hbm.1), custom_call_target="tpu_custom_call" | custom-call | flops 99999997952 | bytes 10000000 | tf_op jit(solution)/shard_map/pallas_call | solution.py:210
  36.0 0.0 collective-permute-done.b_ref
  36.1 0.0 collective-permute-done.5.wo2_ref
  36.1 0.0 collective-permute-done.4.w2_ref
  36.1 0.0 copy-done
  36.1 0.0 copy-done.1
  36.1 2.9 %shard_map.56 = (bf16[64,3072]{1,0:T(8,128)(2,1)S(1)}, bf16[64,3072]{1,0:T(8,128)(2,1)S(1)}, bf16[128,768]{1,0:T(8,128)(2,1)S(1)}, bf16[128,768]{1,0:T(8,128)(2,...) custom-call(s32[1]{0:T(128)} %bitcast.local_ref, ...), custom_call_target="tpu_custom_call" | custom-call | flops 4000000000 | bytes 8000000 | tf_op jit(solution)/shard_map/pallas_call | solution.py:223
  39.0 1.3 %collective-permute-start.6 = (bf16[64,3072]{1,0:T(8,128)(2,1)S(1)}, bf16[64,3072]{1,0:T(8,128)(2,1)S(1)}, u32[]{:S(2)}, u32[]{:S(2)}) collective-permute-start(bf16[64,3072]{1,0:T(8,128)(2,1)S(1)} %get-tuple-element.27), channel_id=1, source_target_pairs={{2,1},{0,3},{7,5},{5,7},{10,9},{8,11},{15,13},{13,15},{18,17},{16,... | collective-permute-start | bytes 1179656 | tf_op jit(solution)/shard_map/ppermute | solution.py:40
  40.3 1.3 %collective-permute-start.7 = (bf16[64,3072]{1,0:T(8,128)(2,1)S(1)}, bf16[64,3072]{1,0:T(8,128)(2,1)S(1)}, u32[]{:S(2)}, u32[]{:S(2)}) collective-permute-start(bf16[64,3072]{1,0:T(8,128)(2,1)S(1)} %get-tuple-element.28), channel_id=1, source_target_pairs={{0,1},{2,3},{5,4},{7,6},{8,9},{10,11},{13,12},{15,14},{16,17},{18,... | collective-permute-start | bytes 1179656 | tf_op jit(solution)/shard_map/ppermute | solution.py:40
  41.6 0.0 collective-permute-done.8.far_a_ref
  41.6 0.0 collective-permute-done.9.far_b_ref
  41.6 4.8 %shard_map.57 = (bf16[64,3072]{1,0:T(8,128)(2,1)S(1)}, bf16[64,3072]{1,0:T(8,128)(2,1)S(1)}, bf16[128,768]{1,0:T(8,128)(2,1)S(1)}, bf16[128,768]{1,0:T(8,128)(2,1)S(1)}) custom-call(s32[1]{0:T(128)} %bitcast.local_ref, bf16[64,3072]{1,0:T(8,128)(2,1)S(1)} %collective-permute-done.8.far_a_ref, bf16[64,3072]{1,0:T(8,128)(2,1)S(1)} %collective-permute-done.9.far_b_ref, ...), custom_call_target="tpu_custom_call" | custom-call | flops 3000000000 | bytes 1000000 | tf_op jit(solution)/shard_map/pallas_call | solution.py:238
  46.4 5.0 %collective-permute-start.11 = (bf16[64,3072]{1,0:T(8,128)(2,1)S(1)}, bf16[64,3072]{1,0:T(8,128)(2,1)S(1)}, u32[]{:S(2)}, u32[]{:S(2)}) collective-permute-start(bf16[64,3072]{1,0:T(8,128)(2,1)S(1)} %get-tuple-element.41), channel_id=1, source_target_pairs={{4,2},{6,0},{1,7},{3,5},{12,10},{14,8},{9,15},{11,13},{20,18},{22,... | collective-permute-start | bytes 1179656 | tf_op jit(solution)/shard_map/ppermute | solution.py:40
  51.4 3.6 %collective-permute-start.12 = (bf16[64,3072]{1,0:T(8,128)(2,1)S(1)}, bf16[64,3072]{1,0:T(8,128)(2,1)S(1)}, u32[]{:S(2)}, u32[]{:S(2)}) collective-permute-start(bf16[64,3072]{1,0:T(8,128)(2,1)S(1)} %get-tuple-element.42), channel_id=1, source_target_pairs={{4,6},{6,4},{1,3},{3,1},{12,14},{14,12},{9,11},{11,9},{20,22},{22,... | collective-permute-start | bytes 1179656 | tf_op jit(solution)/shard_map/ppermute | solution.py:40
  55.0 1.8 %collective-permute-done.6 = bf16[64,3072]{1,0:T(8,128)(2,1)S(1)} collective-permute-done((bf16[64,3072]{1,0:T(8,128)(2,1)S(1)}, bf16[64,3072]{1,0:T(8,128)(2,1)S(1)}, u32[]{:S(2)}, u32[]{:S(2)}) %collective-permute-start.6) | collective-permute-done | bytes 393248 | tf_op jit(solution)/shard_map/ppermute | solution.py:40
  56.8 0.0 collective-permute-done.7
  56.8 2.0 %shard_map.58 = (bf16[64,3072]{1,0:T(8,128)(2,1)S(1)}, bf16[64,3072]{1,0:T(8,128)(2,1)S(1)}) custom-call(bf16[128,768]{1,0:T(8,128)(2,1)S(1)} %get-tuple-element.29.queries, bf16[128,768]{1,0:T(8,128)(2,1)S(1)} %get-tuple-element.30.near_keys, bf16[128,768]{1,0:T(8,128)(2,1)S(1)} %get-tuple-element.31.near_values, ...), custom_call_target="tpu_custom_call" | custom-call | flops 1000000000 | bytes 1000000 | tf_op jit(solution)/shard_map/pallas_call | solution.py:253
  58.8 2.0 %collective-permute-start.10 = (bf16[64,3072]{1,0:T(8,128)(2,1)S(1)}, bf16[64,3072]{1,0:T(8,128)(2,1)S(1)}, u32[]{:S(2)}, u32[]{:S(2)}) collective-permute-start(bf16[64,3072]{1,0:T(8,128)(2,1)S(1)} %get-tuple-element.37), channel_id=1, source_target_pairs={{6,0},{4,2},{3,4},{1,6},{14,8},{12,10},{11,12},{9,14},{22,16},{20,... | collective-permute-start | bytes 1179656 | tf_op jit(solution)/shard_map/ppermute | solution.py:40
  60.9 0.0 collective-permute-done.11
  60.9 3.9 %collective-permute-done.12 = bf16[64,3072]{1,0:T(8,128)(2,1)S(1)} collective-permute-done((bf16[64,3072]{1,0:T(8,128)(2,1)S(1)}, bf16[64,3072]{1,0:T(8,128)(2,1)S(1)}, u32[]{:S(2)}, u32[]{:S(2)}) %collective-permute-start.12) | collective-permute-done | bytes 393248 | tf_op jit(solution)/shard_map/ppermute | solution.py:40
  64.8 0.1 add_convert_fusion.1
  65.0 1.9 %collective-permute-start.13 = (bf16[64,3072]{1,0:T(8,128)(2,1)S(1)}, bf16[64,3072]{1,0:T(8,128)(2,1)S(1)}, u32[]{:S(2)}, u32[]{:S(2)}) collective-permute-start(bf16[64,3072]{1,0:T(8,128)(2,1)S(1)} %add_convert_fusion.1), channel_id=1, source_target_pairs={{2,0},{6,1},{0,2},{4,3},{7,4},{3,5},{5,6},{1,7},{10,8},{14,9},{8,1... | collective-permute-start | bytes 1179656 | tf_op jit(solution)/shard_map/ppermute | solution.py:40
  66.9 2.4 %collective-permute-done.10 = bf16[64,3072]{1,0:T(8,128)(2,1)S(1)} collective-permute-done((bf16[64,3072]{1,0:T(8,128)(2,1)S(1)}, bf16[64,3072]{1,0:T(8,128)(2,1)S(1)}, u32[]{:S(2)}, u32[]{:S(2)}) %collective-permute-start.10) | collective-permute-done | bytes 393248 | tf_op jit(solution)/shard_map/ppermute | solution.py:40
  69.3 0.2 convert_add_fusion
  69.5 10.5 %collective-permute-done.13 = bf16[64,3072]{1,0:T(8,128)(2,1)S(1)} collective-permute-done((bf16[64,3072]{1,0:T(8,128)(2,1)S(1)}, bf16[64,3072]{1,0:T(8,128)(2,1)S(1)}, u32[]{:S(2)}, u32[]{:S(2)}) %collective-permute-start.13) | collective-permute-done | bytes 393248 | tf_op jit(solution)/shard_map/ppermute | solution.py:40
  80.0 0.8 %add_convert_fusion = bf16[64,3072]{1,0:T(8,128)(2,1)} fusion(f32[64,3072]{1,0:T(8,128)S(1)} %convert_add_fusion, bf16[64,3072]{1,0:T(8,128)(2,1)S(1)} %collective-permute-done.13), kind=kLoop, calls=%fused_computation | loop fusion | flops 589824 | bytes 1572864 | tf_op jit(solution)/shard_map/convert_element_type | solution.py:268
Async XLA Ops:
  0.0 20.5 %collective-permute-start.1 = (bf16[64,3072]{1,0:T(8,128)(2,1)}, bf16[64,3072]{1,0:T(8,128)(2,1)S(1)}, u32[]{:S(2)}, u32[]{:S(2)}) collective-permute-start(bf16[64,3072]{1,0:T(8,128)(2,1)} %own_ref.1), channel_id=1, source_target_pairs={{1,0},{3,2},{4,5},{6,7},{9,8},{11,10},{12,13},{14,15},{17,16},{19,... | collective-permute-start | bytes 1179656 | tf_op jit(solution)/shard_map/ppermute | solution.py:40
  2.6 20.4 %collective-permute-start.3 = (bf16[64,3072]{1,0:T(8,128)(2,1)}, bf16[64,3072]{1,0:T(8,128)(2,1)S(1)}, u32[]{:S(2)}, u32[]{:S(2)}) collective-permute-start(bf16[64,3072]{1,0:T(8,128)(2,1)} %own_ref.1), channel_id=1, source_target_pairs={{0,2},{1,6},{2,0},{3,4},{4,7},{5,3},{6,5},{7,1},{8,10},{9,14},{10,... | collective-permute-start | bytes 1179656 | tf_op jit(solution)/shard_map/ppermute | solution.py:40
  8.4 15.9 %collective-permute-start.2 = (f32[2,3,128]{2,1,0:T(4,128)S(1)}, f32[2,3,128]{2,1,0:T(4,128)S(1)}, u32[]{:S(2)}, u32[]{:S(2)}) collective-permute-start(f32[2,3,128]{2,1,0:T(4,128)S(1)} %copy.7.qk_ref), channel_id=1, source_target_pairs={{0,1},{1,0},{2,3},{3,2},{4,5},{5,4},{6,7},{7,6},{8,9},{9,8},{10,11... | collective-permute-start | bytes 9224 | tf_op jit(solution)/shard_map/ppermute | solution.py:40
  15.8 20.2 %collective-permute-start = (bf16[64,3072]{1,0:T(8,128)(2,1)}, bf16[64,3072]{1,0:T(8,128)(2,1)S(1)}, u32[]{:S(2)}, u32[]{:S(2)}) collective-permute-start(bf16[64,3072]{1,0:T(8,128)(2,1)} %own_ref.1), channel_id=1, source_target_pairs={{0,6},{1,2},{2,4},{3,0},{4,3},{5,7},{6,1},{7,5},{8,14},{9,10},{10,... | collective-permute-start | bytes 1179656 | tf_op jit(solution)/shard_map/ppermute | solution.py:40
  18.5 17.6 %collective-permute-start.5 = (bf16[384,3072]{1,0:T(8,128)(2,1)}, bf16[384,3072]{1,0:T(8,128)(2,1)S(1)}, u32[]{:S(2)}, u32[]{:S(2)}) collective-permute-start(bf16[384,3072]{1,0:T(8,128)(2,1)} %wo_hbm.1), channel_id=1, source_target_pairs={{0,1},{1,0},{2,3},{3,2},{4,5},{5,4},{6,7},{7,6},{8,9},{9,8},{10,11... | collective-permute-start | bytes 7077896 | tf_op jit(solution)/shard_map/ppermute | solution.py:40
  20.5 15.6 %copy-start = (bf16[64,3072]{1,0:T(8,128)(2,1)S(1)}, bf16[64,3072]{1,0:T(8,128)(2,1)}, u32[]{:S(2)}) copy-start(bf16[64,3072]{1,0:T(8,128)(2,1)} %own_ref.1) | copy-start | bytes 1179652
  20.5 15.6 %copy-start.1 = (f32[3072]{0:T(1024)S(1)}, f32[3072]{0:T(1024)}, u32[]{:S(2)}) copy-start(f32[3072]{0:T(1024)} %param.6) | copy-start | bytes 36868
  20.5 15.6 %collective-permute-start.4 = (bf16[3072,1152]{1,0:T(8,128)(2,1)}, bf16[3072,1152]{1,0:T(8,128)(2,1)S(1)}, u32[]{:S(2)}, u32[]{:S(2)}) collective-permute-start(bf16[3072,1152]{1,0:T(8,128)(2,1)} %w_hbm.1), channel_id=1, source_target_pairs={{0,1},{1,0},{2,3},{3,2},{4,5},{5,4},{6,7},{7,6},{8,9},{9,8},{10,11... | collective-permute-start | bytes 21233672 | tf_op jit(solution)/shard_map/ppermute | solution.py:40
  23.1 18.5 %collective-permute-start.8 = (bf16[64,3072]{1,0:T(8,128)(2,1)S(1)}, bf16[64,3072]{1,0:T(8,128)(2,1)S(1)}, u32[]{:S(2)}, u32[]{:S(2)}) collective-permute-start(bf16[64,3072]{1,0:T(8,128)(2,1)S(1)} %collective-permute-done.3.a_ref.near_ref), channel_id=1, source_target_pairs={{2,4},{0,6},{7,1},{5,3},{10,12},{8,14},{15,9},{13,11},{18,20},{16,... | collective-permute-start | bytes 1179656 | tf_op jit(solution)/shard_map/ppermute | solution.py:40
  24.4 17.2 %collective-permute-start.9 = (bf16[64,3072]{1,0:T(8,128)(2,1)S(1)}, bf16[64,3072]{1,0:T(8,128)(2,1)S(1)}, u32[]{:S(2)}, u32[]{:S(2)}) collective-permute-start(bf16[64,3072]{1,0:T(8,128)(2,1)S(1)} %collective-permute-done.3.a_ref.near_ref), channel_id=1, source_target_pairs={{6,4},{4,6},{3,1},{1,3},{14,12},{12,14},{11,9},{9,11},{22,20},{20,... | collective-permute-start | bytes 1179656 | tf_op jit(solution)/shard_map/ppermute | solution.py:40
  39.0 17.9 %collective-permute-start.6 = (bf16[64,3072]{1,0:T(8,128)(2,1)S(1)}, bf16[64,3072]{1,0:T(8,128)(2,1)S(1)}, u32[]{:S(2)}, u32[]{:S(2)}) collective-permute-start(bf16[64,3072]{1,0:T(8,128)(2,1)S(1)} %get-tuple-element.27), channel_id=1, source_target_pairs={{2,1},{0,3},{7,5},{5,7},{10,9},{8,11},{15,13},{13,15},{18,17},{16,... | collective-permute-start | bytes 1179656 | tf_op jit(solution)/shard_map/ppermute | solution.py:40
  40.3 16.6 %collective-permute-start.7 = (bf16[64,3072]{1,0:T(8,128)(2,1)S(1)}, bf16[64,3072]{1,0:T(8,128)(2,1)S(1)}, u32[]{:S(2)}, u32[]{:S(2)}) collective-permute-start(bf16[64,3072]{1,0:T(8,128)(2,1)S(1)} %get-tuple-element.28), channel_id=1, source_target_pairs={{0,1},{2,3},{5,4},{7,6},{8,9},{10,11},{13,12},{15,14},{16,17},{18,... | collective-permute-start | bytes 1179656 | tf_op jit(solution)/shard_map/ppermute | solution.py:40
  46.4 14.5 %collective-permute-start.11 = (bf16[64,3072]{1,0:T(8,128)(2,1)S(1)}, bf16[64,3072]{1,0:T(8,128)(2,1)S(1)}, u32[]{:S(2)}, u32[]{:S(2)}) collective-permute-start(bf16[64,3072]{1,0:T(8,128)(2,1)S(1)} %get-tuple-element.41), channel_id=1, source_target_pairs={{4,2},{6,0},{1,7},{3,5},{12,10},{14,8},{9,15},{11,13},{20,18},{22,... | collective-permute-start | bytes 1179656 | tf_op jit(solution)/shard_map/ppermute | solution.py:40
  51.4 13.4 %collective-permute-start.12 = (bf16[64,3072]{1,0:T(8,128)(2,1)S(1)}, bf16[64,3072]{1,0:T(8,128)(2,1)S(1)}, u32[]{:S(2)}, u32[]{:S(2)}) collective-permute-start(bf16[64,3072]{1,0:T(8,128)(2,1)S(1)} %get-tuple-element.42), channel_id=1, source_target_pairs={{4,6},{6,4},{1,3},{3,1},{12,14},{14,12},{9,11},{11,9},{20,22},{22,... | collective-permute-start | bytes 1179656 | tf_op jit(solution)/shard_map/ppermute | solution.py:40
  58.8 10.5 %collective-permute-start.10 = (bf16[64,3072]{1,0:T(8,128)(2,1)S(1)}, bf16[64,3072]{1,0:T(8,128)(2,1)S(1)}, u32[]{:S(2)}, u32[]{:S(2)}) collective-permute-start(bf16[64,3072]{1,0:T(8,128)(2,1)S(1)} %get-tuple-element.37), channel_id=1, source_target_pairs={{6,0},{4,2},{3,4},{1,6},{14,8},{12,10},{11,12},{9,14},{22,16},{20,... | collective-permute-start | bytes 1179656 | tf_op jit(solution)/shard_map/ppermute | solution.py:40
  65.0 15.1 %collective-permute-start.13 = (bf16[64,3072]{1,0:T(8,128)(2,1)S(1)}, bf16[64,3072]{1,0:T(8,128)(2,1)S(1)}, u32[]{:S(2)}, u32[]{:S(2)}) collective-permute-start(bf16[64,3072]{1,0:T(8,128)(2,1)S(1)} %add_convert_fusion.1), channel_id=1, source_target_pairs={{2,0},{6,1},{0,2},{4,3},{7,4},{3,5},{5,6},{1,7},{10,8},{14,9},{8,1... | collective-permute-start | bytes 1179656 | tf_op jit(solution)/shard_map/ppermute | solution.py:40
